TPU v7x, 256 devices: a whole 4x4x8 slice. The times are simulated.
256 devices in a mesh: grp: 8 (over z), enc: 32 (over y, x, core).
Axes of the slice: x: 4, y: 4, z: 8, core: 2. Of those that a mesh axis runs over, the one named last changes fastest.
Arguments:
- history: bfloat16 [3072, 128, 1024], P(('grp', 'enc')), may hold values from -6 to 6
- hist_len: int32 [3072], P(('grp', 'enc')), may hold values from 0 to 2, as said below
- cand: bfloat16 [131072, 1024], P(('grp', 'enc')), may hold values from -6 to 6
- cand_owner: int32 [131072, 1], P(('grp', 'enc')), may hold values from 0 to 255; in each aligned block of 512 rows (0 to 511, 512 to 1023, ...) at most 3 rows name the same one
- cand_user: int32 [131072], P(('grp', 'enc')), may hold values from 0 to 11
- norm_gain: float32 [1024], replicated, may hold values from 0.1 to 1.9
- w_proj: bfloat16 [1024, 2048], replicated, may hold values from -0.1875 to 0.1875
Outputs:
- kv_cache: bfloat16 [3072, 128, 1024], P(('grp', 'enc'))
- cand_out: bfloat16 [131072, 512], P(('grp', 'enc'))
Inputs may be any that keep to these rules, and one draw needn't show every extreme that they name: `hist_len`: blocks of history of each missed user; the first user slot of every device has 2. `cand_owner`: among the 512 candidates of one device no owner device is named more than 3 times.
All inputs are finite; a program needn't handle non-finite values.
Results may differ from a plain program's by a relative error of at most 0.013.
Values may be sent and summed in bfloat16 or wider, within the bound.
A program may use at most 64 MiB of HBM per device.

v0:
```python
import jax
import jax.numpy as jnp
from jax import lax
from jax.sharding import PartitionSpec as P

HDIM = 128
PIECE = 64


def norm_rows(values):
    center = values - jnp.mean(values, axis=-1, keepdims=True)
    spread = jnp.mean(center * center, axis=-1, keepdims=True)
    return center * lax.rsqrt(spread + 1e-05)


def attend(query, own_k, own_v, uid, keys_leading_layout, values_leading_layout, col_user):
    count = query.shape[0]
    width = query.shape[1]
    heads = width // HDIM
    score_scale = HDIM ** (-0.5)
    query_per_head = query.reshape(count, heads, HDIM)
    scores = (
        jnp.einsum(
            "ofk,fgk->fog", query_per_head, keys_leading_layout, preferred_element_type=jnp.float32
        )
        * score_scale
    )
    belongs = col_user[None, None, :] == uid[None, :, None]
    attention_weight = jnp.where(belongs, jax.nn.silu(scores), 0.0).astype(jnp.bfloat16)
    self_score = jnp.sum(
        query_per_head.astype(jnp.float32) * own_k.reshape(count, heads, HDIM).astype(jnp.float32),
        axis=-1,
    )
    self_weight = jax.nn.silu(self_score * score_scale).astype(jnp.bfloat16)
    reduced_total = jnp.einsum(
        "tlc,tcf->ltf", attention_weight, values_leading_layout, preferred_element_type=jnp.float32
    )
    reduced_total = reduced_total + self_weight.astype(jnp.float32)[:, :, None] * own_v.reshape(
        count, heads, HDIM
    ).astype(jnp.float32)
    return norm_rows(reduced_total.reshape(count, width)).astype(jnp.bfloat16)


def project_rows(rows_in, norm_gain, w_proj):
    normed = (norm_rows(rows_in.astype(jnp.float32)) * norm_gain).astype(jnp.bfloat16)
    return jax.nn.silu(jnp.dot(normed, w_proj, preferred_element_type=jnp.float32)).astype(
        jnp.bfloat16
    )


def body(history, hist_len, cand, cand_owner, cand_user, norm_gain, w_proj):
    rows = history.shape[1]
    width = w_proj.shape[1] // 4
    heads = width // HDIM
    n_enc = lax.axis_size("enc")
    n_grp = lax.axis_size("grp")
    n_dev = n_grp * n_enc
    w_kv = jnp.concatenate([w_proj[:, 3 * width :], w_proj[:, width : 2 * width]], axis=1)
    normed_hist = (norm_rows(history.astype(jnp.float32)) * norm_gain).astype(jnp.bfloat16)
    mixed = jnp.einsum("urd,de->ure", normed_hist, w_kv, preferred_element_type=jnp.float32)
    keyval = jax.nn.silu(mixed).astype(jnp.bfloat16)
    row_ids = jnp.arange(rows, dtype=jnp.int32)
    live_rows = row_ids[None, :] < (hist_len * PIECE)[:, None]
    kv_cache = jnp.where(live_rows[:, :, None], keyval, jnp.zeros((), keyval.dtype))
    user_slots = kv_cache.shape[0]
    flat_kv = kv_cache.reshape(user_slots * rows, 2 * width)
    keys_leading_layout = (
        flat_kv[:, :width].reshape(user_slots * rows, heads, HDIM).transpose(1, 0, 2)
    )
    values_leading_layout = (
        flat_kv[:, width:].reshape(user_slots * rows, heads, HDIM).transpose(1, 0, 2)
    )
    col_user = jnp.arange(user_slots * rows, dtype=jnp.int32) // rows
    count = cand.shape[0]
    cap_cand = max(2, 3 * count // (2 * n_dev))
    owners = cand_owner[:, 0]
    cand_ids = jnp.arange(count, dtype=jnp.int32)
    same_owner = owners[:, None] == owners[None, :]
    cand_rank = jnp.sum(same_owner & (cand_ids[None, :] < cand_ids[:, None]), axis=1)
    dev_ids = jnp.arange(n_dev, dtype=jnp.int32)
    cslot_ids = jnp.arange(cap_cand, dtype=jnp.int32)
    ctable = (owners[None, None, :] == dev_ids[:, None, None]) & (
        cand_rank[None, None, :] == cslot_ids[None, :, None]
    )
    slot_cand = jnp.sum(jnp.where(ctable, cand_ids[None, None, :], 0), axis=2)
    candidate_slot_active = jnp.any(ctable, axis=2)
    slot_uid = jnp.where(candidate_slot_active, cand_user[slot_cand], 0)
    slot_uid = slot_uid.reshape(n_grp, n_enc, cap_cand)
    dest_grp = owners // n_enc
    dest_enc = owners % n_enc
    total_slots = n_dev * cap_cand
    block = 128
    cand_buf = jnp.where(
        candidate_slot_active[:, :, None], cand[slot_cand], jnp.zeros((), cand.dtype)
    )
    cand_buf = cand_buf.reshape(n_grp, n_enc, cap_cand, cand.shape[1])
    arrived, arrived_uid = (
        lax.all_to_all(
            lax.all_to_all(cand_buf, "grp", split_axis=0, concat_axis=0, tiled=True),
            "enc",
            split_axis=1,
            concat_axis=1,
            tiled=True,
        ),
        lax.all_to_all(
            lax.all_to_all(slot_uid, "grp", split_axis=0, concat_axis=0, tiled=True),
            "enc",
            split_axis=1,
            concat_axis=1,
            tiled=True,
        ),
    )

    def per_block(item):
        rows_in, uid = item
        projected = project_rows(rows_in, norm_gain, w_proj)
        normed_attn = attend(
            projected[:, 2 * width : 3 * width],
            projected[:, 3 * width :],
            projected[:, width : 2 * width],
            uid,
            keys_leading_layout,
            values_leading_layout,
            col_user,
        )
        return (normed_attn.astype(jnp.float32) * projected[:, :width].astype(jnp.float32)).astype(
            jnp.bfloat16
        )

    flat_in = arrived.reshape(total_slots // block, block, cand.shape[1])
    flat_uid = arrived_uid.reshape(total_slots // block, block)
    result = lax.map(per_block, (flat_in, flat_uid)).reshape(n_grp, n_enc, cap_cand, width)
    answered = lax.all_to_all(
        lax.all_to_all(result, "grp", split_axis=0, concat_axis=0, tiled=True),
        "enc",
        split_axis=1,
        concat_axis=1,
        tiled=True,
    )
    cand_out = answered[dest_grp, dest_enc, cand_rank]
    return (kv_cache, cand_out)


def solution(mesh):
    placed = (
        P(("grp", "enc"), None, None),
        P(("grp", "enc")),
        P(("grp", "enc"), None),
        P(("grp", "enc"), None),
        P(("grp", "enc")),
        P(),
        P(),
    )
    return jax.shard_map(
        body,
        mesh=mesh,
        in_specs=placed,
        out_specs=(P(("grp", "enc"), None, None), P(("grp", "enc"), None)),
        check_vma=False,
    )
```

profile of v0, /device:TPU:1, one launch (start us, length us, event | category | flops | bytes accessed | tf_op | source)
XLA Modules:
  0.0 242.4 jit_solution(6382201800794087588)
XLA Ops:
  0.7 1.0 convert_reduce_fusion.2
  1.7 0.8 iota_compare_fusion.1
  3.6 5.0 %gather_fusion = s32[768]{0:T(1024)S(1)} fusion(s32[512]{0:T(512)S(1)} %copy-done.1, s32[1024]{0:T(1024)S(1)} %pad_clamp_fusion), kind=kCustom, calls=%fused_computation | custom fusion | bytes 9216 | tf_op jit(solution)/shard_map/gather | solution.py:87
  8.8 0.7 copy.76
  9.6 9.0 %all-to-all-start = ((s32[8,32,3]{1,2,0:T(4,128)}), s32[8,32,3]{1,2,0:T(4,128)S(1)}, u32[]{:S(2)}, u32[]{:S(2)}) async-start(s32[8,32,3]{1,2,0:T(4,128)} %copy.76), calls=%async_computation | async-start | bytes 32768 | tf_op jit(solution)/shard_map/all_to_all | solution.py:106
  18.6 2.8 %gather_fusion.1 = bf16[768,1024]{1,0:T(8,128)(2,1)S(1)} fusion(bf16[512,1024]{1,0:T(8,128)(2,1)S(1)} %copy-done, s32[1024]{0:T(1024)S(1)} %pad_clamp_fusion), kind=kCustom, calls=%fused_computation.1 | custom fusion | bytes 3148800 | tf_op jit(solution)/shard_map/gather | solution.py:94
  21.4 2.3 gather.16
  23.7 2.4 broadcast_select_fusion
  26.1 1.8 copy.80
  27.9 6.6 %all-to-all-start.2 = ((bf16[8,32,3,1024]{3,1,2,0:T(8,128)(2,1)}), bf16[8,32,3,1024]{3,1,2,0:T(8,128)(2,1)S(1)}, u32[]{:S(2)}, u32[]{:S(2)}) async-start(bf16[8,32,3,1024]{3,1,2,0:T(8,128)(2,1)} %copy.80), calls=%async_computation.2 | async-start | bytes 3145728 | tf_op jit(solution)/shard_map/all_to_all | solution.py:99
  34.5 2.5 %convert_reduce_fusion.1 = f32[12,128]{1,0:T(8,128)S(1)} fusion(bf16[12,128,1024]{2,1,0:T(8,128)(2,1)} %param.9), kind=kLoop, calls=%fused_computation.56 | loop fusion | flops 3144192 | bytes 3151872 | tf_op jit(solution)/shard_map/reduce_sum | solution.py:11
  37.3 1.0 fusion.37
  38.3 3.0 %fusion.65 = (bf16[1024,512]{1,0:T(8,128)(2,1)}, bf16[1024,512]{1,0:T(8,128)(2,1)}) fusion(bf16[1024,2048]{1,0:T(8,128)(2,1)} %param.15), kind=kLoop, calls=%fused_computation.106 | loop fusion | bytes 4194304 | tf_op jit(solution)/shard_map/slice | solution.py:58
  41.4 0.7 copy.77
  42.1 30.7 %all-to-all-done.2 = bf16[8,32,3,1024]{3,1,2,0:T(8,128)(2,1)S(1)} async-done(((bf16[8,32,3,1024]{3,1,2,0:T(8,128)(2,1)}), bf16[8,32,3,1024]{3,1,2,0:T(8,128)(2,1)S(1)}, u32[]{:S(2)}, u32[]{:S(2)}) %all-to-all-start.2) | async-done | bytes 1572896 | tf_op jit(solution)/shard_map/all_to_all | solution.py:99
  72.8 9.8 %all-to-all-start.1 = ((s32[8,32,3]{0,2,1:T(4,128)}), s32[8,32,3]{0,2,1:T(4,128)S(1)}, u32[]{:S(2)}, u32[]{:S(2)}) async-start(s32[8,32,3]{0,2,1:T(4,128)} %copy.77), calls=%async_computation.1 | async-start | bytes 131072 | tf_op jit(solution)/shard_map/all_to_all | solution.py:105
  82.6 2.0 copy.81
  84.7 5.2 %all-to-all-done.1 = s32[8,32,3]{0,2,1:T(4,128)S(1)} async-done(((s32[8,32,3]{0,2,1:T(4,128)}), s32[8,32,3]{0,2,1:T(4,128)S(1)}, u32[]{:S(2)}, u32[]{:S(2)}) %all-to-all-start.1) | async-done | bytes 3104 | tf_op jit(solution)/shard_map/all_to_all | solution.py:105
  89.9 4.7 %all-to-all-start.3 = ((bf16[8,32,3,1024]{3,0,2,1:T(8,128)(2,1)}), bf16[8,32,3,1024]{3,0,2,1:T(8,128)(2,1)}, u32[]{:S(2)}, u32[]{:S(2)}) async-start(bf16[8,32,3,1024]{3,0,2,1:T(8,128)(2,1)} %copy.81), calls=%async_computation.3 | async-start | bytes 3145728 | tf_op jit(solution)/shard_map/all_to_all | solution.py:98
  94.6 6.0 %fusion.45 = bf16[12,128,1024]{2,1,0:T(8,128)(2,1)S(1)} fusion(pred[12,128]{1,0:T(8,128)(4,1)S(1)} %iota_compare_fusion.3, bf16[12,128,1024]{2,1,0:T(8,128)(2,1)} %param.9, f32[1024]{0:T(1024)S(1)} %copy-done.7, f32[12,128]{1,0:T(8,128)S(1)} %add_rsqrt_fusion.2, f32[12,128]{1,0:T(8,128)S(1)} %broadcast_multiply_fusion.2, ...), kind=kOutput, calls=%fused_computation.67 | convolution fusion | flops 3242721280 | bytes 8406528 | tf_op jit(solution)/shard_map/urd,de->ure/dot_general | solution.py:60
  100.7 2.1 fusion.66
  103.3 1.7 copy.92
  105.0 1.6 copy.85
  106.6 2.6 %copy.84 = bf16[1536,512]{0,1:T(8,128)(2,1)} copy(bf16[1536,512]{1,0:T(8,128)(2,1)} %get-tuple-element.132) | data formatting | bytes 3145728 | tf_op jit(solution)/shard_map/slice | solution.py:71
  109.7 7.1 %all-to-all-done.3 = bf16[8,32,3,1024]{3,0,2,1:T(8,128)(2,1)} async-done(((bf16[8,32,3,1024]{3,0,2,1:T(8,128)(2,1)}), bf16[8,32,3,1024]{3,0,2,1:T(8,128)(2,1)}, u32[]{:S(2)}, u32[]{:S(2)}) %all-to-all-start.3) | async-done | bytes 1572896 | tf_op jit(solution)/shard_map/all_to_all | solution.py:98
  116.8 2.8 %copy.82 = bf16[8,32,3,1024]{3,2,1,0:T(4,128)(2,1)S(1)} copy(bf16[8,32,3,1024]{3,0,2,1:T(8,128)(2,1)} %all-to-all-done.3) | data formatting | bytes 3145728 | tf_op jit(solution)/shard_map/all_to_all | solution.py:98
  119.5 2.5 %reshape.229 = bf16[6,128,1024]{2,1,0:T(8,128)(2,1)} reshape(bf16[8,32,3,1024]{3,2,1,0:T(4,128)(2,1)S(1)} %copy.82) | data formatting | bytes 3145728 | tf_op jit(solution)/shard_map/reshape | solution.py:130
  122.0 65.2 %while.11 = (s32[]{:T(128)}, bf16[6,128,512]{2,1,0:T(8,128)(2,1)}, s32[6,128]{1,0:T(8,128)S(1)}, bf16[6,128,1024]{2,1,0:T(8,128)(2,1)}, f32[1024]{0:T(1024)S(1)}...) while((s32[]{:T(128)}, bf16[6,128,512]{2,1,0:T(8,128)(2,1)}, ...), condition=%wide.region_11.12_spmd.clone, body=%wide.region_5.11_spmd.clone.sunk | while | flops 949173504 | bytes 13934185 | solution.py:132
  122.0 1.1 convert_reduce_fusion.4
  123.1 1.2 fusion.86
  124.3 3.2 %multiply_convert_fusion.5 = bf16[128,2048]{1,0:T(8,128)(2,1)S(1)} fusion(bf16[1024,2048]{1,0:T(8,128)(2,1)} %get-tuple-element.218, f32[1024]{0:T(1024)S(1)} %get-tuple-element.217, f32[128]{0:T(128)S(1)} %add_rsqrt_fusion.5, f32[128]{0:T(128)S(1)} %broadcast_multiply_fusion.6, bf16[6,128,1024]{2,1,0:T(8,128)(2,1)} %get-tuple-element.216, ...), kind=kOutput, calls=%fused_computation.9.clone.1 | convolution fusion | flops 538836992 | bytes 4986368 | tf_op jit(solution)/shard_map/while/body/eval_jaxpr/dot_general | solution.py:46
  128.3 3.5 %fusion.90 = (f32[128]{0:T(128)S(1)}, f32[128,4,128]{0,2,1:T(8,128)S(1)}) fusion(f32[128,4,128]{0,2,1:T(8,128)S(1)} %bitcast.80, f32[128,4]{0,1:T(4,128)S(1)} %fusion.88, bf16[4,1536,128]{1,2,0:T(8,128)(2,1)} %get-tuple-element.220, bf16[4,1536,128]{2,1,0:T(8,128)(2,1)} %get-tuple-element.219, pred[128,1536]{1,0:T(8,128)(4,1)S(1)} %broadcast_compare_fusion.2, ...), kind=kOutput, calls=%fused_computation.105.clone.1 | convolution fusion | flops 408354688 | bytes 4000256 | tf_op jit(solution)/shard_map/while/body/eval_jaxpr/tlc,tcf->ltf/dot_general | solution.py:35
  132.1 0.8 fusion.91
  132.9 1.1 convert_reduce_fusion.4
  134.0 1.2 fusion.86
  135.1 3.2 %multiply_convert_fusion.5 = bf16[128,2048]{1,0:T(8,128)(2,1)S(1)} fusion(bf16[1024,2048]{1,0:T(8,128)(2,1)} %get-tuple-element.218, f32[1024]{0:T(1024)S(1)} %get-tuple-element.217, f32[128]{0:T(128)S(1)} %add_rsqrt_fusion.5, f32[128]{0:T(128)S(1)} %broadcast_multiply_fusion.6, bf16[6,128,1024]{2,1,0:T(8,128)(2,1)} %get-tuple-element.216, ...), kind=kOutput, calls=%fused_computation.9.clone.1 | convolution fusion | flops 538836992 | bytes 4986368 | tf_op jit(solution)/shard_map/while/body/eval_jaxpr/dot_general | solution.py:46
  139.2 3.5 %fusion.90 = (f32[128]{0:T(128)S(1)}, f32[128,4,128]{0,2,1:T(8,128)S(1)}) fusion(f32[128,4,128]{0,2,1:T(8,128)S(1)} %bitcast.80, f32[128,4]{0,1:T(4,128)S(1)} %fusion.88, bf16[4,1536,128]{1,2,0:T(8,128)(2,1)} %get-tuple-element.220, bf16[4,1536,128]{2,1,0:T(8,128)(2,1)} %get-tuple-element.219, pred[128,1536]{1,0:T(8,128)(4,1)S(1)} %broadcast_compare_fusion.2, ...), kind=kOutput, calls=%fused_computation.105.clone.1 | convolution fusion | flops 408354688 | bytes 4000256 | tf_op jit(solution)/shard_map/while/body/eval_jaxpr/tlc,tcf->ltf/dot_general | solution.py:35
  143.0 0.8 fusion.91
  143.7 1.1 convert_reduce_fusion.4
  144.8 1.2 fusion.86
  146.0 3.2 %multiply_convert_fusion.5 = bf16[128,2048]{1,0:T(8,128)(2,1)S(1)} fusion(bf16[1024,2048]{1,0:T(8,128)(2,1)} %get-tuple-element.218, f32[1024]{0:T(1024)S(1)} %get-tuple-element.217, f32[128]{0:T(128)S(1)} %add_rsqrt_fusion.5, f32[128]{0:T(128)S(1)} %broadcast_multiply_fusion.6, bf16[6,128,1024]{2,1,0:T(8,128)(2,1)} %get-tuple-element.216, ...), kind=kOutput, calls=%fused_computation.9.clone.1 | convolution fusion | flops 538836992 | bytes 4986368 | tf_op jit(solution)/shard_map/while/body/eval_jaxpr/dot_general | solution.py:46
  150.0 3.5 %fusion.90 = (f32[128]{0:T(128)S(1)}, f32[128,4,128]{0,2,1:T(8,128)S(1)}) fusion(f32[128,4,128]{0,2,1:T(8,128)S(1)} %bitcast.80, f32[128,4]{0,1:T(4,128)S(1)} %fusion.88, bf16[4,1536,128]{1,2,0:T(8,128)(2,1)} %get-tuple-element.220, bf16[4,1536,128]{2,1,0:T(8,128)(2,1)} %get-tuple-element.219, pred[128,1536]{1,0:T(8,128)(4,1)S(1)} %broadcast_compare_fusion.2, ...), kind=kOutput, calls=%fused_computation.105.clone.1 | convolution fusion | flops 408354688 | bytes 4000256 | tf_op jit(solution)/shard_map/while/body/eval_jaxpr/tlc,tcf->ltf/dot_general | solution.py:35
  153.8 0.8 fusion.91
  154.6 1.1 convert_reduce_fusion.4
  155.7 1.2 fusion.86
  156.9 3.2 %multiply_convert_fusion.5 = bf16[128,2048]{1,0:T(8,128)(2,1)S(1)} fusion(bf16[1024,2048]{1,0:T(8,128)(2,1)} %get-tuple-element.218, f32[1024]{0:T(1024)S(1)} %get-tuple-element.217, f32[128]{0:T(128)S(1)} %add_rsqrt_fusion.5, f32[128]{0:T(128)S(1)} %broadcast_multiply_fusion.6, bf16[6,128,1024]{2,1,0:T(8,128)(2,1)} %get-tuple-element.216, ...), kind=kOutput, calls=%fused_computation.9.clone.1 | convolution fusion | flops 538836992 | bytes 4986368 | tf_op jit(solution)/shard_map/while/body/eval_jaxpr/dot_general | solution.py:46
  160.9 3.5 %fusion.90 = (f32[128]{0:T(128)S(1)}, f32[128,4,128]{0,2,1:T(8,128)S(1)}) fusion(f32[128,4,128]{0,2,1:T(8,128)S(1)} %bitcast.80, f32[128,4]{0,1:T(4,128)S(1)} %fusion.88, bf16[4,1536,128]{1,2,0:T(8,128)(2,1)} %get-tuple-element.220, bf16[4,1536,128]{2,1,0:T(8,128)(2,1)} %get-tuple-element.219, pred[128,1536]{1,0:T(8,128)(4,1)S(1)} %broadcast_compare_fusion.2, ...), kind=kOutput, calls=%fused_computation.105.clone.1 | convolution fusion | flops 408354688 | bytes 4000256 | tf_op jit(solution)/shard_map/while/body/eval_jaxpr/tlc,tcf->ltf/dot_general | solution.py:35
  164.7 0.8 fusion.91
  165.5 1.1 convert_reduce_fusion.4
  166.6 1.2 fusion.86
  167.7 3.2 %multiply_convert_fusion.5 = bf16[128,2048]{1,0:T(8,128)(2,1)S(1)} fusion(bf16[1024,2048]{1,0:T(8,128)(2,1)} %get-tuple-element.218, f32[1024]{0:T(1024)S(1)} %get-tuple-element.217, f32[128]{0:T(128)S(1)} %add_rsqrt_fusion.5, f32[128]{0:T(128)S(1)} %broadcast_multiply_fusion.6, bf16[6,128,1024]{2,1,0:T(8,128)(2,1)} %get-tuple-element.216, ...), kind=kOutput, calls=%fused_computation.9.clone.1 | convolution fusion | flops 538836992 | bytes 4986368 | tf_op jit(solution)/shard_map/while/body/eval_jaxpr/dot_general | solution.py:46
  171.8 3.5 %fusion.90 = (f32[128]{0:T(128)S(1)}, f32[128,4,128]{0,2,1:T(8,128)S(1)}) fusion(f32[128,4,128]{0,2,1:T(8,128)S(1)} %bitcast.80, f32[128,4]{0,1:T(4,128)S(1)} %fusion.88, bf16[4,1536,128]{1,2,0:T(8,128)(2,1)} %get-tuple-element.220, bf16[4,1536,128]{2,1,0:T(8,128)(2,1)} %get-tuple-element.219, pred[128,1536]{1,0:T(8,128)(4,1)S(1)} %broadcast_compare_fusion.2, ...), kind=kOutput, calls=%fused_computation.105.clone.1 | convolution fusion | flops 408354688 | bytes 4000256 | tf_op jit(solution)/shard_map/while/body/eval_jaxpr/tlc,tcf->ltf/dot_general | solution.py:35
  175.6 0.8 fusion.91
  176.4 1.1 convert_reduce_fusion.4
  177.4 1.2 fusion.86
  178.6 3.2 %multiply_convert_fusion.5 = bf16[128,2048]{1,0:T(8,128)(2,1)S(1)} fusion(bf16[1024,2048]{1,0:T(8,128)(2,1)} %get-tuple-element.218, f32[1024]{0:T(1024)S(1)} %get-tuple-element.217, f32[128]{0:T(128)S(1)} %add_rsqrt_fusion.5, f32[128]{0:T(128)S(1)} %broadcast_multiply_fusion.6, bf16[6,128,1024]{2,1,0:T(8,128)(2,1)} %get-tuple-element.216, ...), kind=kOutput, calls=%fused_computation.9.clone.1 | convolution fusion | flops 538836992 | bytes 4986368 | tf_op jit(solution)/shard_map/while/body/eval_jaxpr/dot_general | solution.py:46
  182.7 3.5 %fusion.90 = (f32[128]{0:T(128)S(1)}, f32[128,4,128]{0,2,1:T(8,128)S(1)}) fusion(f32[128,4,128]{0,2,1:T(8,128)S(1)} %bitcast.80, f32[128,4]{0,1:T(4,128)S(1)} %fusion.88, bf16[4,1536,128]{1,2,0:T(8,128)(2,1)} %get-tuple-element.220, bf16[4,1536,128]{2,1,0:T(8,128)(2,1)} %get-tuple-element.219, pred[128,1536]{1,0:T(8,128)(4,1)S(1)} %broadcast_compare_fusion.2, ...), kind=kOutput, calls=%fused_computation.105.clone.1 | convolution fusion | flops 408354688 | bytes 4000256 | tf_op jit(solution)/shard_map/while/body/eval_jaxpr/tlc,tcf->ltf/dot_general | solution.py:35
  186.5 0.8 fusion.91
  187.2 2.4 %reshape.233 = bf16[8,32,3,512]{3,2,1,0:T(4,128)(2,1)S(1)} reshape(bf16[6,128,512]{2,1,0:T(8,128)(2,1)} %get-tuple-element.49) | data formatting | bytes 1572864 | tf_op jit(solution)/shard_map/reshape | solution.py:132
  189.9 22.6 %all_to_all.30 = bf16[8,32,3,512]{3,1,2,0:T(8,128)(2,1)S(1)} all-to-all(bf16[8,32,3,512]{3,1,2,0:T(8,128)(2,1)S(1)} %copy.86), channel_id=1, replica_groups=mesh['grp'=8,'enc'=32] {'grp'}, dimensions={0} | all-to-all | bytes 1572864 | tf_op jit(solution)/shard_map/all_to_all | solution.py:134
  212.5 1.3 copy.87
  213.8 8.4 %all-to-all-start.5 = ((bf16[8,32,3,512]{3,0,2,1:T(8,128)(2,1)}), bf16[8,32,3,512]{3,0,2,1:T(8,128)(2,1)S(1)}, u32[]{:S(2)}, u32[]{:S(2)}) async-start(bf16[8,32,3,512]{3,0,2,1:T(8,128)(2,1)} %copy.87), calls=%async_computation.5 | async-start | bytes 1572864 | tf_op jit(solution)/shard_map/all_to_all | solution.py:133
  222.3 14.2 %all-to-all-done.5 = bf16[8,32,3,512]{3,0,2,1:T(8,128)(2,1)S(1)} async-done(((bf16[8,32,3,512]{3,0,2,1:T(8,128)(2,1)}), bf16[8,32,3,512]{3,0,2,1:T(8,128)(2,1)S(1)}, u32[]{:S(2)}, u32[]{:S(2)}) %all-to-all-start.5) | async-done | bytes 786464 | tf_op jit(solution)/shard_map/all_to_all | solution.py:133
  236.7 5.7 %gather_fusion.2 = bf16[512,512]{1,0:T(8,128)(2,1)} fusion(bf16[8,32,3,512]{3,1,2,0:T(8,128)(2,1)S(1)} %copy.88, s32[512]{0:T(512)S(1)} %bitcast.78), kind=kCustom, calls=%fused_computation.2 | custom fusion | bytes 1054720 | tf_op jit(solution)/shard_map/gather | solution.py:140
  (135 shorter events, 9.6 us)
Async XLA Ops:
  0.6 18.0 %copy-start = (bf16[512,1024]{1,0:T(8,128)(2,1)S(1)}, bf16[512,1024]{1,0:T(8,128)(2,1)}, u32[]{:S(2)}) copy-start(bf16[512,1024]{1,0:T(8,128)(2,1)} %param.11) | copy-start | bytes 3145732
  0.6 2.9 %copy-start.1 = (s32[512]{0:T(512)S(1)}, s32[512]{0:T(512)}, u32[]{:S(2)}) copy-start(s32[512]{0:T(512)} %param.13) | copy-start | bytes 6148
  9.6 18.3 %all-to-all-start = ((s32[8,32,3]{1,2,0:T(4,128)}), s32[8,32,3]{1,2,0:T(4,128)S(1)}, u32[]{:S(2)}, u32[]{:S(2)}) async-start(s32[8,32,3]{1,2,0:T(4,128)} %copy.76), calls=%async_computation | async-start | bytes 32768 | tf_op jit(solution)/shard_map/all_to_all | solution.py:106
  26.1 8.4 %copy-start.8 = (s32[12]{0:T(128)S(1)}, s32[12]{0:T(128)}, u32[]{:S(2)}) copy-start(s32[12]{0:T(128)} %param.10) | copy-start | bytes 148
  27.9 44.9 %all-to-all-start.2 = ((bf16[8,32,3,1024]{3,1,2,0:T(8,128)(2,1)}), bf16[8,32,3,1024]{3,1,2,0:T(8,128)(2,1)S(1)}, u32[]{:S(2)}, u32[]{:S(2)}) async-start(bf16[8,32,3,1024]{3,1,2,0:T(8,128)(2,1)} %copy.80), calls=%async_computation.2 | async-start | bytes 3145728 | tf_op jit(solution)/shard_map/all_to_all | solution.py:99
  34.5 2.8 %copy-start.2 = (bf16[12,128,1024]{2,1,0:T(8,128)(2,1)S(1)}, bf16[12,128,1024]{2,1,0:T(8,128)(2,1)}, u32[]{:S(2)}) copy-start(bf16[12,128,1024]{2,1,0:T(8,128)(2,1)} %param.9) | copy-start | bytes 9437188
  72.8 17.1 %all-to-all-start.1 = ((s32[8,32,3]{0,2,1:T(4,128)}), s32[8,32,3]{0,2,1:T(4,128)S(1)}, u32[]{:S(2)}, u32[]{:S(2)}) async-start(s32[8,32,3]{0,2,1:T(4,128)} %copy.77), calls=%async_computation.1 | async-start | bytes 131072 | tf_op jit(solution)/shard_map/all_to_all | solution.py:105
  82.6 12.0 %copy-start.7 = (f32[1024]{0:T(1024)S(1)}, f32[1024]{0:T(1024)}, u32[]{:S(2)}) copy-start(f32[1024]{0:T(1024)} %param.14) | copy-start | bytes 12292
  84.7 9.9 %copy-start.4 = (bf16[1024,512]{1,0:T(8,128)(2,1)S(1)}, bf16[1024,512]{1,0:T(8,128)(2,1)}, u32[]{:S(2)}) copy-start(bf16[1024,512]{1,0:T(8,128)(2,1)} %get-tuple-element.130) | copy-start | bytes 3145732
  84.7 9.9 %copy-start.5 = (bf16[1024,512]{1,0:T(8,128)(2,1)S(1)}, bf16[1024,512]{1,0:T(8,128)(2,1)}, u32[]{:S(2)}) copy-start(bf16[1024,512]{1,0:T(8,128)(2,1)} %get-tuple-element.131) | copy-start | bytes 3145732
  89.9 26.9 %all-to-all-start.3 = ((bf16[8,32,3,1024]{3,0,2,1:T(8,128)(2,1)}), bf16[8,32,3,1024]{3,0,2,1:T(8,128)(2,1)}, u32[]{:S(2)}, u32[]{:S(2)}) async-start(bf16[8,32,3,1024]{3,0,2,1:T(8,128)(2,1)} %copy.81), calls=%async_computation.3 | async-start | bytes 3145728 | tf_op jit(solution)/shard_map/all_to_all | solution.py:98
  100.6 2.7 %copy-start.3 = (bf16[12,128,1024]{2,1,0:T(8,128)(2,1)}, bf16[12,128,1024]{2,1,0:T(8,128)(2,1)S(1)}, u32[]{:S(2)}) copy-start(bf16[12,128,1024]{2,1,0:T(8,128)(2,1)S(1)} %fusion.45) | copy-start | bytes 9437188
  189.7 32.6 %copy-start.6 = (s32[512,1]{0,1:T(1,128)S(1)}, s32[512,1]{0,1:T(1,128)}, u32[]{:S(2)}) copy-start(s32[512,1]{0,1:T(1,128)} %param.12) | copy-start | bytes 6148
  213.8 22.7 %all-to-all-start.5 = ((bf16[8,32,3,512]{3,0,2,1:T(8,128)(2,1)}), bf16[8,32,3,512]{3,0,2,1:T(8,128)(2,1)S(1)}, u32[]{:S(2)}, u32[]{:S(2)}) async-start(bf16[8,32,3,512]{3,0,2,1:T(8,128)(2,1)} %copy.87), calls=%async_computation.5 | async-start | bytes 1572864 | tf_op jit(solution)/shard_map/all_to_all | solution.py:133
where the time goes:
time: 244 us; the launch traced here: 242 us
  waiting for transfers between devices  57.1 us (23%)
  local copies, waits for them, and re-layouts  46.5 us (19%)
  matrix products  46.2 us (19%)
  starting transfers between devices  38.6 us (16%)
  other arithmetic  29.9 us (12%)
  blocking collectives  22.6 us (9%)
    all_to_all x1, waiting for transfers between devices, body(): lax.all_to_all(cand_buf, 'grp', split_axis=0, concat_axis=0, tiled=True)  30.7 us
    all_to_all x1, blocking collectives, body(): lax.all_to_all(result, 'grp', split_axis=0, concat_axis=0, tiled=True)  22.6 us
    dot_general x6, matrix products, attend(): jnp.einsum('tlc,tcf->ltf', attention_weight, values_leading_layout, prefe...  21.3 us
    dot_general x6, matrix products, project_rows(): jnp.dot(normed, w_proj, preferred_element_type=jnp.float32)  19 us
    all_to_all x1, waiting for transfers between devices, body(): lax.all_to_all(lax.all_to_all(result, 'grp', split_axis=0, concat_axis=0,...  14.2 us
    all_to_all x1, starting transfers between devices, body(): lax.all_to_all(lax.all_to_all(slot_uid, 'grp', split_axis=0, concat_axis=...  9.78 us
    all_to_all x1, starting transfers between devices, body(): lax.all_to_all(slot_uid, 'grp', split_axis=0, concat_axis=0, tiled=True)  9.01 us
    reduce_sum x7, other arithmetic, norm_rows(): center = values - jnp.mean(values, axis=-1, keepdims=True)  8.91 us
  transfers between devices with their start and end apart: 5, of which 4 were waited for; matrix products, arithmetic and copies ran while one was open for 14% of the time, Pallas kernels for 0%

commit v1 on v0

v1 whole, which is shorter than its diff:
```python
import functools

import jax
import jax.numpy as jnp
from jax import lax
from jax.experimental import pallas as pl
from jax.experimental.pallas import tpu as pltpu
from jax.sharding import PartitionSpec as P

MESH = pl.DeviceIdType.MESH
HDIM = 128
HEADS = 4
HD = 512
D = 1024
PIECE = 64
ROWS = 128
USERS = 12
CAND = 512
CAP = 3
CHIPS = 128
GROUPS = 4
GSIZE = 32
QROWS = 32
RROWS = 24
BF = jnp.bfloat16
F32 = jnp.float32


def silu(x):
    half = 0.5 * x
    return half + half * jnp.tanh(half)


def norm_rows(x):
    center = x - jnp.mean(x, axis=-1, keepdims=True)
    spread = jnp.mean(center * center, axis=-1, keepdims=True)
    return center * lax.rsqrt(spread + 1e-5)


def dot(a, b):
    return jnp.dot(a, b, preferred_element_type=F32)


def dot_t(a, b):
    return lax.dot_general(a, b, (((1,), (1,)), ((), ())), preferred_element_type=F32)


def kernel(
    len_ref, owner_ref, user_ref, gain_ref, cand_hbm, hist_hbm, w_hbm,
    kv_hbm, out_ref,
    cand_v, hist_v, w_v, kv_v, xn_v, q_v, u_v, self_v, pick_v, place_v,
    tab_own, tab_sib, msg, sib_out, sib_in, land, land_f, ret_f, ret_msg, ret_land, ret_sib,
    back_own, back_sib, back_v,
    load_sem, kv_sem, sib_send, sib_recv, ready_sem,
    q_send, q_recv, r_send, r_recv, f_send, f_recv,
):
    g, e = lax.axis_index("grp"), lax.axis_index("enc")
    y, x, c = e // 8, (e // 2) % 4, e % 2
    sibling = (g, y * 8 + x * 2 + 1 - c)

    def plane_peer(k):
        return g, ((y + k // 4) % 4) * 8 + ((x + k % 4) % 4) * 2 + c

    def peer(idx, sign):
        grp, half, k = idx // 32, (idx // 16) % 2, idx % 16
        dz = (1 - half) * ((4 - grp) % 4) + half * (4 + grp)
        py = (y + sign * (k // 4) + 4) % 4
        px = (x + sign * (k % 4) + 4) % 4
        return (g + sign * dz + 8) % 8, py * 8 + px * 2 + c

    cols = [(2 * HD, 3 * HD), (3 * HD, 4 * HD), (HD, 2 * HD), (0, HD)]
    loads = [pltpu.make_async_copy(cand_hbm, cand_v, load_sem.at[0])]
    for i, (lo, hi) in enumerate(cols):
        loads.append(
            pltpu.make_async_copy(
                w_hbm.at[:, pl.ds(lo, HD)], w_v.at[:, pl.ds(lo, HD)], load_sem.at[1 + i]
            )
        )
    loads.append(pltpu.make_async_copy(hist_hbm, hist_v, load_sem.at[5]))
    for i in (0, 1, 5, 2, 3, 4):
        loads[i].start()

    barrier = pltpu.get_barrier_semaphore()

    def greet_ring(k, carry):
        pl.semaphore_signal(
            barrier, inc=1, device_id=((g + k) % 8, e), device_id_type=MESH
        )
        return carry

    def greet_plane(k, carry):
        pl.semaphore_signal(barrier, inc=1, device_id=plane_peer(k), device_id_type=MESH)
        return carry

    lax.fori_loop(1, 8, greet_ring, 0)
    lax.fori_loop(1, 16, greet_plane, 0)
    pl.semaphore_signal(barrier, inc=1, device_id=sibling, device_id_type=MESH)

    rows_i = lax.broadcasted_iota(jnp.int32, (CAND, CAND), 0)
    cols_i = lax.broadcasted_iota(jnp.int32, (CAND, CAND), 1)
    owner_col = owner_ref[...]
    owner_f = owner_col.astype(F32)
    owner_row = jnp.sum(jnp.where(rows_i == cols_i, owner_f, 0.0), axis=0, keepdims=True)
    same = (owner_f == owner_row) & (cols_i < rows_i)
    rank = jnp.sum(jnp.where(same, 1.0, 0.0), axis=1, keepdims=True).astype(jnp.int32)
    to_g, to_e = owner_col // 32, owner_col % 32
    dz = (to_g - g + 8) % 8
    half = dz // 4
    grp = jnp.where(half == 1, dz - 4, (4 - dz) % 4)
    ry = (to_e // 8 - y + 4) % 4
    rx = ((to_e // 2) % 4 - x + 4) % 4
    other = jnp.where(to_e % 2 == c, 0, 1)
    code_col = (other * CAP + rank) * CHIPS + grp * 32 + half * 16 + ry * 4 + rx
    code_f = code_col.astype(F32)
    code_row = jnp.sum(jnp.where(rows_i == cols_i, code_f, 0.0), axis=0, keepdims=True)
    user_f = user_ref[...].astype(F32)
    user_col = jnp.sum(jnp.where(rows_i == cols_i, user_f, 0.0), axis=1, keepdims=True)
    user_mat = jnp.broadcast_to(user_col, (CAND, HDIM)).astype(BF)
    lane_slot = lax.broadcasted_iota(jnp.int32, (CAND, 2 * CAP * CHIPS), 1).astype(F32)
    place_v[...] = jnp.where(lane_slot == code_f, 1.0, 0.0).astype(BF)
    sub_slot = lax.broadcasted_iota(jnp.int32, (2 * CAP * CHIPS, CAND), 0).astype(F32)
    pick_v[...] = jnp.where(sub_slot == code_row, 1.0, 0.0).astype(BF)

    gain = gain_ref[...]
    loads[0].wait()
    loads[1].wait()

    def query_step(i, carry):
        at = pl.ds(pl.multiple_of(i * 256, 256), 256)
        xn = (norm_rows(cand_v[at, :].astype(F32)) * gain).astype(BF)
        xn_v[at, :] = xn
        q_v[at, :] = silu(dot(xn, w_v[:, 2 * HD : 3 * HD])).astype(BF)
        return carry

    lax.fori_loop(0, 2, query_step, 0)

    tab_own[...] = jnp.zeros_like(tab_own)
    tab_sib[...] = jnp.zeros_like(tab_sib)
    for m, tab in ((1, tab_sib), (0, tab_own)):
        for s in range(CAP):
            first = (m * CAP + s) * CHIPS
            pick = pick_v[first : first + CHIPS, :]
            got = dot(pick, q_v[...])
            for h in range(HEADS):
                tab[pl.ds(c * 12 + h * CAP + s, CHIPS, stride=QROWS), :] = got[
                    :, h * HDIM : (h + 1) * HDIM
                ]
            tab[pl.ds(24 + c * CAP + s, CHIPS, stride=QROWS), :] = dot(pick, user_mat)
    sib_out[...] = tab_sib[...].astype(BF).reshape(CHIPS, QROWS, HDIM)

    pl.semaphore_wait(barrier, 23)
    swap = pltpu.make_async_remote_copy(
        src_ref=sib_out, dst_ref=sib_in, send_sem=sib_send, recv_sem=sib_recv,
        device_id=sibling, device_id_type=MESH,
    )
    swap.start()

    def say_ready(k, carry):
        pl.semaphore_signal(ready_sem, inc=1, device_id=plane_peer(k), device_id_type=MESH)
        return carry

    lax.fori_loop(1, 16, say_ready, 0)
    own = tab_own[...].astype(BF).reshape(CHIPS, QROWS, HDIM)
    msg[...] = own
    swap.wait()
    msg[...] = msg[...] + sib_in[...]
    pl.semaphore_wait(ready_sem, 15)

    land[0] = msg[0]

    def send_query(j, carry):
        grp = j // 32
        idx = grp * 32 + (j % 2) * 16 + (j % 32) // 2
        pltpu.make_async_remote_copy(
            src_ref=msg.at[idx], dst_ref=land.at[idx],
            send_sem=q_send.at[grp], recv_sem=q_recv.at[grp],
            device_id=peer(idx, 1), device_id_type=MESH,
        ).start()
        return carry

    lax.fori_loop(1, CHIPS, send_query, 0)

    loads[2].wait()
    loads[3].wait()
    loads[5].wait()

    def encode_step(i, carry):
        at = pl.ds(pl.multiple_of(i * 256, 256), 256)
        xn = (norm_rows(hist_v[at, :].astype(F32)) * gain).astype(BF)
        row = lax.broadcasted_iota(jnp.int32, (256, HD), 0)
        live = row < jnp.where(
            row < ROWS, len_ref[2 * i] * PIECE, len_ref[2 * i + 1] * PIECE + ROWS
        )
        keys = silu(dot(xn, w_v[:, 3 * HD :]))
        kv_v[at, :HD] = jnp.where(live, keys, 0.0).astype(BF)
        values = silu(dot(xn, w_v[:, HD : 2 * HD]))
        kv_v[at, HD:] = jnp.where(live, values, 0.0).astype(BF)
        pltpu.make_async_copy(kv_v.at[at, :], kv_hbm.at[at, :], kv_sem).start()
        return carry

    lax.fori_loop(0, USERS // 2, encode_step, 0)

    def remote_span(grp, ref, sem):
        return pltpu.make_async_copy(
            ref.at[pl.ds(grp * GSIZE, GSIZE)], ref.at[pl.ds(grp * GSIZE, GSIZE)], sem.at[grp]
        )

    def first_span(ref, sem):
        return pltpu.make_async_copy(
            ref.at[pl.ds(1, GSIZE - 1)], ref.at[pl.ds(1, GSIZE - 1)], sem.at[0]
        )

    half_scale = 0.5 * HDIM**-0.5

    def attend_group(grp):
        land_f[...] = land[pl.ds(grp * GSIZE, GSIZE)].astype(F32).reshape(GSIZE * QROWS, HDIM)
        uid = jnp.concatenate(
            [land_f[pl.ds(24 + j, GSIZE, stride=QROWS), :] for j in range(2 * CAP)], axis=0
        )
        for h in range(HEADS):
            query = jnp.concatenate(
                [
                    land_f[pl.ds(cs * 12 + h * CAP + s, GSIZE, stride=QROWS), :]
                    for cs in range(2)
                    for s in range(CAP)
                ],
                axis=0,
            ).astype(BF)
            total = None
            for pair in range(USERS // 2):
                at = slice(pair * 256, pair * 256 + 256)
                score = dot_t(query, kv_v[at, h * HDIM : (h + 1) * HDIM]) * half_scale
                weight = score + score * jnp.tanh(score)
                mine = jnp.concatenate([uid == 2.0 * pair, uid == 2.0 * pair + 1.0], axis=1)
                weight = jnp.where(mine, weight, 0.0).astype(BF)
                part = dot(weight, kv_v[at, HD + h * HDIM : HD + (h + 1) * HDIM])
                total = part if total is None else total + part
            for j in range(2 * CAP):
                row = (j // CAP) * 12 + h * CAP + j % CAP
                ret_f[pl.ds(row, GSIZE, stride=RROWS), :] = total[j * GSIZE : (j + 1) * GSIZE, :]
        ret_msg[pl.ds(grp * GSIZE, GSIZE)] = ret_f[...].reshape(GSIZE, RROWS, HDIM).astype(BF)

    def send_back(j, carry):
        grp = j // 32
        idx = grp * 32 + (j % 2) * 16 + (j % 32) // 2
        pltpu.make_async_remote_copy(
            src_ref=ret_msg.at[idx], dst_ref=ret_land.at[idx],
            send_sem=r_send.at[grp], recv_sem=r_recv.at[grp],
            device_id=peer(idx, -1), device_id_type=MESH,
        ).start()
        return carry

    first_span(land, q_recv).wait()
    attend_group(0)
    ret_land[0] = ret_msg[0]
    lax.fori_loop(1, 32, send_back, 0)

    def group_step(grp, carry):
        remote_span(grp, land, q_recv).wait()
        attend_group(grp)
        lax.fori_loop(grp * 32, grp * 32 + 32, send_back, 0)
        return carry

    lax.fori_loop(1, GROUPS, group_step, 0)

    loads[4].wait()

    def own_step(i, carry):
        at = pl.ds(pl.multiple_of(i * 256, 256), 256)
        xn = xn_v[at, :]
        u_v[at, :] = silu(dot(xn, w_v[:, :HD])).astype(BF)
        own_v = silu(dot(xn, w_v[:, HD : 2 * HD])).astype(BF).astype(F32)
        own_k = silu(dot(xn, w_v[:, 3 * HD :])).astype(BF).astype(F32)
        prod = q_v[at, :].astype(F32) * own_k
        for h in range(HEADS):
            lanes = slice(h * HDIM, (h + 1) * HDIM)
            score = jnp.sum(prod[:, lanes], axis=-1, keepdims=True) * half_scale
            weight = (score + score * jnp.tanh(score)).astype(BF).astype(F32)
            self_v[at, lanes] = weight * own_v[:, lanes]
        return carry

    lax.fori_loop(0, 2, own_step, 0)

    def hand_on(grp):
        span = pl.ds(grp * GSIZE, GSIZE)
        return pltpu.make_async_remote_copy(
            src_ref=ret_land.at[span], dst_ref=ret_sib.at[span],
            send_sem=f_send.at[grp], recv_sem=f_recv.at[grp],
            device_id=sibling, device_id_type=MESH,
        )

    first_span(ret_land, r_recv).wait()
    hand_on(0).start()

    def hand_step(grp, carry):
        remote_span(grp, ret_land, r_recv).wait()
        hand_on(grp).start()
        return carry

    lax.fori_loop(1, GROUPS, hand_step, 0)
    back_own[...] = ret_land[...].astype(F32).reshape(CHIPS * RROWS, HDIM)

    def hand_wait(grp, carry):
        hand_on(grp).wait()
        return carry

    lax.fori_loop(0, GROUPS, hand_wait, 0)
    back_sib[...] = ret_sib[...].astype(F32).reshape(CHIPS * RROWS, HDIM)
    for m, back in ((0, back_own), (1, back_sib)):
        for s in range(CAP):
            first = (m * CAP + s) * CHIPS
            for h in range(HEADS):
                back_v[first : first + CHIPS, h * HDIM : (h + 1) * HDIM] = back[
                    pl.ds(c * 12 + h * CAP + s, CHIPS, stride=RROWS), :
                ].astype(BF)

    def out_step(i, carry):
        at = pl.ds(pl.multiple_of(i * 256, 256), 256)
        attended = dot(place_v[at, :], back_v[...]) + self_v[at, :]
        normed = norm_rows(attended).astype(BF).astype(F32)
        out_ref[at, :] = (normed * u_v[at, :].astype(F32)).astype(BF)
        return carry

    lax.fori_loop(0, 2, out_step, 0)

    first_span(msg, q_send).wait()
    first_span(ret_msg, r_send).wait()

    def sent(grp, carry):
        remote_span(grp, msg, q_send).wait()
        remote_span(grp, ret_msg, r_send).wait()
        return carry

    lax.fori_loop(1, GROUPS, sent, 0)
    pltpu.make_async_copy(kv_v, kv_hbm, kv_sem).wait()


def body(history, hist_len, cand, cand_owner, cand_user, norm_gain, w_proj):
    any_spec = pl.BlockSpec(memory_space=pl.ANY)
    vmem = pl.BlockSpec(memory_space=pltpu.VMEM)
    dma = pltpu.SemaphoreType.DMA
    kv, out = pl.pallas_call(
        kernel,
        out_shape=(
            jax.ShapeDtypeStruct((USERS * ROWS, 2 * HD), BF),
            jax.ShapeDtypeStruct((CAND, HD), BF),
        ),
        in_specs=[
            pl.BlockSpec(memory_space=pltpu.SMEM), vmem, vmem, vmem, any_spec, any_spec, any_spec,
        ],
        out_specs=(any_spec, vmem),
        scratch_shapes=[
            pltpu.VMEM((CAND, D), BF),
            pltpu.VMEM((USERS * ROWS, D), BF),
            pltpu.VMEM((D, 4 * HD), BF),
            pltpu.VMEM((USERS * ROWS, 2 * HD), BF),
            pltpu.VMEM((CAND, D), BF),
            pltpu.VMEM((CAND, HD), BF),
            pltpu.VMEM((CAND, HD), BF),
            pltpu.VMEM((CAND, HD), F32),
            pltpu.VMEM((2 * CAP * CHIPS, CAND), BF),
            pltpu.VMEM((CAND, 2 * CAP * CHIPS), BF),
            pltpu.VMEM((CHIPS * QROWS, HDIM), F32),
            pltpu.VMEM((CHIPS * QROWS, HDIM), F32),
            pltpu.VMEM((CHIPS, QROWS, HDIM), BF),
            pltpu.VMEM((CHIPS, QROWS, HDIM), BF),
            pltpu.VMEM((CHIPS, QROWS, HDIM), BF),
            pltpu.VMEM((CHIPS, QROWS, HDIM), BF),
            pltpu.VMEM((GSIZE * QROWS, HDIM), F32),
            pltpu.VMEM((GSIZE * RROWS, HDIM), F32),
            pltpu.VMEM((CHIPS, RROWS, HDIM), BF),
            pltpu.VMEM((CHIPS, RROWS, HDIM), BF),
            pltpu.VMEM((CHIPS, RROWS, HDIM), BF),
            pltpu.VMEM((CHIPS * RROWS, HDIM), F32),
            pltpu.VMEM((CHIPS * RROWS, HDIM), F32),
            pltpu.VMEM((2 * CAP * CHIPS, HD), BF),
            dma((6,)),
            dma,
            dma,
            dma,
            pltpu.SemaphoreType.REGULAR,
            dma((GROUPS,)),
            dma((GROUPS,)),
            dma((GROUPS,)),
            dma((GROUPS,)),
            dma((GROUPS,)),
            dma((GROUPS,)),
        ],
        compiler_params=pltpu.CompilerParams(
            collective_id=0, has_side_effects=True, vmem_limit_bytes=56 << 20
        ),
        cost_estimate=pl.CostEstimate(
            flops=12_000_000_000, bytes_accessed=12_000_000, transcendentals=8_000_000
        ),
        name="routed_attention",
    )(
        hist_len,
        cand_owner,
        cand_user.reshape(1, CAND),
        norm_gain.reshape(1, D),
        cand,
        history.reshape(USERS * ROWS, D),
        w_proj,
    )
    return kv.reshape(USERS, ROWS, 2 * HD), out


def solution(mesh):
    placed = (
        P(("grp", "enc"), None, None),
        P(("grp", "enc")),
        P(("grp", "enc"), None),
        P(("grp", "enc"), None),
        P(("grp", "enc")),
        P(),
        P(),
    )
    return jax.shard_map(
        body,
        mesh=mesh,
        in_specs=placed,
        out_specs=(P(("grp", "enc"), None, None), P(("grp", "enc"), None)),
        check_vma=False,
    )
```

time: 244 us -> 73.2 us (0.30)
  Pallas kernels: 0 us -> 66.2 us
  waiting for transfers between devices: 57.1 us -> 0 us
  matrix products: 46.2 us -> 0 us
  local copies, waits for them, and re-layouts: 46.5 us -> 6.25 us
  starting transfers between devices: 38.6 us -> 0 us
  other arithmetic: 29.9 us -> 0 us
  blocking collectives: 22.6 us -> 0 us
    pallas_call x0 -> x1, Pallas kernels: none -> 66.2 us  [body(): pl.pallas_call(kernel, out_shape=(jax.ShapeDtypeStruct((USERS * ROWS, 2 *...]
    all_to_all x5 -> x0, waiting for transfers between devices: 57.1 us -> none  [the longest x1 30.7 us: body(): lax.all_to_all(cand_buf, 'grp', split_axis=0, concat_axis=0, tiled=True)]
    dot_general x13 -> x0, matrix products: 46.2 us -> none  [the longest x6 21.3 us: attend(): jnp.einsum('tlc,tcf->ltf', attention_weight, values_leading_layout, prefe...]
    all_to_all x5 -> x0, starting transfers between devices: 38.6 us -> none  [the longest x1 9.78 us: body(): lax.all_to_all(lax.all_to_all(slot_uid, 'grp', split_axis=0, concat_axis=...]
    all_to_all x1 -> x0, blocking collectives: 22.6 us -> none  [body(): lax.all_to_all(result, 'grp', split_axis=0, concat_axis=0, tiled=True)]
    reduce_sum x28 -> x0, other arithmetic: 20.1 us -> none  [the longest x7 8.91 us: norm_rows(): center = values - jnp.mean(values, axis=-1, keepdims=True)]
    gather x5 -> x0, local copies, waits for them, and re-layouts: 16 us -> none  [the longest x1 5.71 us: body(): cand_out = answered[dest_grp, dest_enc, cand_rank]]
    slice x3 -> x0, local copies, waits for them, and re-layouts: 7.73 us -> none  [the longest x2 4.69 us: body(): flat_kv[:, width:].reshape(user_slots * rows, heads, HDIM)]
  transfers between devices with their start and end apart: 5 -> 0, of which waited for: 4 -> 0; matrix products, arithmetic and copies ran while one was open for 14% -> 0% of each run, Pallas kernels for 0% -> 0%
where the time goes in v1:
time: 73.2 us; the launch traced here: 73.1 us
  Pallas kernels  66.2 us (90%)
  local copies, waits for them, and re-layouts  6.25 us (9%)
    pallas_call x1, Pallas kernels, body(): pl.pallas_call(kernel, out_shape=(jax.ShapeDtypeStruct((USERS * ROWS, 2 *...  66.2 us
    unnamed x5, local copies, waits for them, and re-layouts  6.25 us

profile of v1, /device:TPU:1, one launch (start us, length us, event | category | flops | bytes accessed | tf_op | source)
XLA Modules:
  0.0 73.1 jit_solution(2272970237122963224)
XLA Ops:
  0.6 1.5 %copy.9.owner_ref = s32[512,1]{1,0:T(8,128)} copy(s32[512,1]{0,1:T(1,128)} %param.10) | data formatting | bytes 4096 | tf_op args[3]
  2.2 66.2 %routed_attention.1 = (bf16[1536,1024]{1,0:T(8,128)(2,1)}, bf16[512,512]{1,0:T(8,128)(2,1)}) custom-call(s32[12]{0:T(128)} %len_ref.1, s32[512,1]{1,0:T(8,128)} %copy.9.owner_ref, s32[1,512]{1,0:T(1,128)} %bitcast.7, f32[1,1024]{1,0:T(1,128)} %bitcast.6, bf16[512,1024]{1,0:T(8,128)(2,1)} %cand_hbm.1, bf16[1536,1024]{1,0:T(8,128)(2,1)} %bitcast.5, ...), custom_call_target="tpu_custom_call" | custom-call | flops 12000000000 | bytes 12000000 | tf_op jit(solution)/shard_map/routed_attention/pallas_call | solution.py:342
  68.4 0.0 copy-start
  68.4 3.9 %copy.12 = bf16[12,128,1024]{2,1,0:T(8,128)(2,1)} copy(bf16[12,128,1024]{2,1,0:T(8,128)(2,1)} %bitcast.4) | data formatting | bytes 6291456
  72.3 0.0 copy-done
  72.3 0.8 %copy.13 = bf16[512,512]{1,0:T(8,128)(2,1)} copy(bf16[512,512]{1,0:T(8,128)(2,1)S(1)} %copy-done) | data formatting | bytes 1048576
Async XLA Ops:
  68.4 3.9 %copy-start = (bf16[512,512]{1,0:T(8,128)(2,1)S(1)}, bf16[512,512]{1,0:T(8,128)(2,1)}, u32[]{:S(2)}) copy-start(bf16[512,512]{1,0:T(8,128)(2,1)} %get-tuple-element.9) | copy-start | bytes 1572868

commit v2 on v1

v2 whole, which is shorter than its diff:
```python
import functools

import jax
import jax.numpy as jnp
from jax import lax
from jax.experimental import pallas as pl
from jax.experimental.pallas import tpu as pltpu
from jax.sharding import PartitionSpec as P

MESH = pl.DeviceIdType.MESH
HDIM = 128
HEADS = 4
HD = 512
D = 1024
PIECE = 64
ROWS = 128
USERS = 12
CAND = 512
CAP = 3
CHIPS = 128
GROUPS = 4
GSIZE = 32
MROWS = 24
BF = jnp.bfloat16
F32 = jnp.float32


def silu(x):
    half = 0.5 * x
    return half + half * jnp.tanh(half)


def norm_rows(x):
    center = x - jnp.mean(x, axis=-1, keepdims=True)
    spread = jnp.mean(center * center, axis=-1, keepdims=True)
    return center * lax.rsqrt(spread + 1e-5)


def dot(a, b):
    return jnp.dot(a, b, preferred_element_type=F32)


def dot_t(a, b):
    return lax.dot_general(a, b, (((1,), (1,)), ((), ())), preferred_element_type=F32)


def kernel(
    len_ref, owner_ref, user_ref, gain_ref, cand_hbm, hist_hbm, w_hbm,
    kv_hbm, out_ref,
    cand_v, hist_v, w_v, kv_v, xn_v, q_v, u_v, att_v, place_v,
    sib_out, sib_in, tab, msg, land, land_f, ret_f, ret_msg, ret_land, ret_sib, back_f, back_v,
    slot_out, slot_in, ring_out, ring_in, plane_out, plane_in,
    load_sem, kv_sem, sib_send, sib_recv, ready_sem,
    q_send, q_recv, r_send, r_recv, f_send, f_recv, s_send, s_recv,
):
    g, e = lax.axis_index("grp"), lax.axis_index("enc")
    y, x, c = e // 8, (e // 2) % 4, e % 2
    sibling = (g, y * 8 + x * 2 + 1 - c)

    def plane_peer(k):
        return g, ((y + k // 4) % 4) * 8 + ((x + k % 4) % 4) * 2 + c

    def ring_shift(r):
        return (1 - r % 2) * ((4 - r // 2) % 4) + (r % 2) * (4 + r // 2)

    def peer(idx, sign):
        dz, k = ring_shift(idx // 16), idx % 16
        py = (y + sign * (k // 4) + 4) % 4
        px = (x + sign * (k % 4) + 4) % 4
        return (g + sign * dz + 8) % 8, py * 8 + px * 2 + c

    cols = [(2 * HD, 3 * HD), (3 * HD, 4 * HD), (HD, 2 * HD), (0, HD)]
    loads = [pltpu.make_async_copy(cand_hbm, cand_v, load_sem.at[0])]
    for i, (lo, hi) in enumerate(cols):
        loads.append(
            pltpu.make_async_copy(
                w_hbm.at[:, pl.ds(lo, HD)], w_v.at[:, pl.ds(lo, HD)], load_sem.at[1 + i]
            )
        )
    loads.append(pltpu.make_async_copy(hist_hbm, hist_v, load_sem.at[5]))
    for i in (0, 1, 5, 2, 3, 4):
        loads[i].start()

    barrier = pltpu.get_barrier_semaphore()

    def greet_ring(k, carry):
        pl.semaphore_signal(
            barrier, inc=1, device_id=((g + k) % 8, e), device_id_type=MESH
        )
        return carry

    def greet_plane(k, carry):
        pl.semaphore_signal(barrier, inc=1, device_id=plane_peer(k), device_id_type=MESH)
        return carry

    lax.fori_loop(1, 8, greet_ring, 0)
    lax.fori_loop(1, 16, greet_plane, 0)
    pl.semaphore_signal(barrier, inc=1, device_id=sibling, device_id_type=MESH)

    rows_i = lax.broadcasted_iota(jnp.int32, (CAND, CAND), 0)
    cols_i = lax.broadcasted_iota(jnp.int32, (CAND, CAND), 1)
    owner = owner_ref[...]
    owner_f = owner.astype(F32)
    owner_col = jnp.sum(jnp.where(rows_i == cols_i, owner_f, 0.0), axis=1, keepdims=True)
    same = (owner_col == owner_f) & (rows_i < cols_i)
    rank = jnp.sum(jnp.where(same, 1.0, 0.0), axis=0, keepdims=True).astype(jnp.int32)
    to_g, to_e = owner // 32, owner % 32
    dz = (to_g - g + 8) % 8
    half = dz // 4
    grp = jnp.where(half == 1, dz - 4, (4 - dz) % 4)
    ry = (to_e // 8 - y + 4) % 4
    rx = ((to_e // 2) % 4 - x + 4) % 4
    other = jnp.where(to_e % 2 == c, 0, 1)
    shift = ry * 4 + rx
    code = (other * CAP + rank) * CHIPS + grp * 32 + half * 16 + shift

    def pick(j):
        slot = lax.broadcasted_iota(jnp.int32, (CHIPS, CAND), 0) + j * CHIPS
        return jnp.where(slot == code, 1.0, 0.0).astype(BF)

    ring_row = lax.broadcasted_iota(jnp.int32, (8, CAND), 0) + 8 * other
    slot_lane = lax.broadcasted_iota(jnp.int32, (HDIM, CAND), 0)
    lane_hot = jnp.where(slot_lane == (c * CAP + rank) * 16 + shift, 1.0, 0.0).astype(BF)
    user_f = user_ref[...].astype(F32)

    def slot_users(m):
        mine = ring_row == grp * 2 + half + 8 * m
        return dot_t(jnp.where(mine, user_f, 0.0).astype(BF), lane_hot)

    slot_out[...] = slot_users(1)

    gain = gain_ref[...]
    loads[0].wait()
    loads[1].wait()

    def query_step(i, carry):
        at = pl.ds(pl.multiple_of(i * 256, 256), 256)
        xn = (norm_rows(cand_v[at, :].astype(F32)) * gain).astype(BF)
        xn_v[at, :] = xn
        q_v[at, :] = silu(dot(xn, w_v[:, 2 * HD : 3 * HD])).astype(BF)
        return carry

    lax.fori_loop(0, 2, query_step, 0)

    def swap(s):
        return pltpu.make_async_remote_copy(
            src_ref=sib_out.at[s], dst_ref=sib_in.at[s],
            send_sem=sib_send.at[s], recv_sem=sib_recv.at[s],
            device_id=sibling, device_id_type=MESH,
        )

    swap_users = pltpu.make_async_remote_copy(
        src_ref=slot_out, dst_ref=slot_in, send_sem=sib_send.at[CAP], recv_sem=sib_recv.at[CAP],
        device_id=sibling, device_id_type=MESH,
    )

    for s in range(CAP):
        sib_out[s] = dot(pick(CAP + s), q_v[...]).astype(BF)
        if s == 0:
            pl.semaphore_wait(barrier, 23)
            swap_users.start()
        swap(s).start()

    def say_ready(k, carry):
        pl.semaphore_signal(ready_sem, inc=1, device_id=plane_peer(k), device_id_type=MESH)
        return carry

    lax.fori_loop(1, 16, say_ready, 0)

    def lay(rows, core, s):
        for h in range(HEADS):
            tab[pl.ds(core * 12 + h * CAP + s, CHIPS, stride=MROWS), :] = rows[
                :, h * HDIM : (h + 1) * HDIM
            ]

    for s in range(CAP):
        lay(dot(pick(s), q_v[...]), c, s)
    own_users = slot_users(0)
    for s in range(CAP):
        swap(s).wait()
        lay(sib_in[s].astype(F32), 1 - c, s)
    pl.semaphore_wait(ready_sem, 15)

    def send_query(j, carry):
        idx = (j // 32) * 32 + (j % 2) * 16 + (j % 32) // 2
        pltpu.make_async_remote_copy(
            src_ref=msg.at[idx], dst_ref=land.at[idx],
            send_sem=q_send.at[j // 32], recv_sem=q_recv.at[j // 32],
            device_id=peer(idx, 1), device_id_type=MESH,
        ).start()
        return carry

    def fill(grp):
        rows = pl.ds(grp * GSIZE * MROWS, GSIZE * MROWS)
        msg[pl.ds(grp * GSIZE, GSIZE)] = tab[rows, :].reshape(GSIZE, MROWS, HDIM).astype(BF)

    def send_group(grp):
        lax.fori_loop(grp * GSIZE, grp * GSIZE + GSIZE, send_query, 0)

    fill(0)
    lax.fori_loop(1, GSIZE, send_query, 0)
    fill(1)
    send_group(1)
    land[0] = msg[0]
    fill(2)
    fill(3)

    def remote_span(grp, ref, sem):
        return pltpu.make_async_copy(
            ref.at[pl.ds(grp * GSIZE, GSIZE)], ref.at[pl.ds(grp * GSIZE, GSIZE)], sem.at[grp]
        )

    def first_span(ref, sem):
        return pltpu.make_async_copy(
            ref.at[pl.ds(1, GSIZE - 1)], ref.at[pl.ds(1, GSIZE - 1)], sem.at[0]
        )

    swap_users.wait()
    ring_out[...] = (own_users + slot_in[...]).reshape(8, 1, HDIM)
    ring_in[0] = ring_out[0]

    def send_ring(r, carry):
        pltpu.make_async_remote_copy(
            src_ref=ring_out.at[r], dst_ref=ring_in.at[r],
            send_sem=s_send.at[0], recv_sem=s_recv.at[0],
            device_id=((g + ring_shift(r)) % 8, e), device_id_type=MESH,
        ).start()
        return carry

    lax.fori_loop(1, 8, send_ring, 0)

    loads[2].wait()
    loads[3].wait()
    loads[5].wait()

    def encode_step(i, carry):
        at = pl.ds(pl.multiple_of(i * 256, 256), 256)
        xn = (norm_rows(hist_v[at, :].astype(F32)) * gain).astype(BF)
        row = lax.broadcasted_iota(jnp.int32, (256, HD), 0)
        live = row < jnp.where(
            row < ROWS, len_ref[2 * i] * PIECE, len_ref[2 * i + 1] * PIECE + ROWS
        )
        keys = silu(dot(xn, w_v[:, 3 * HD :]))
        kv_v[at, :HD] = jnp.where(live, keys, 0.0).astype(BF)
        values = silu(dot(xn, w_v[:, HD : 2 * HD]))
        kv_v[at, HD:] = jnp.where(live, values, 0.0).astype(BF)
        pltpu.make_async_copy(kv_v.at[at, :], kv_hbm.at[at, :], kv_sem).start()
        return carry

    lax.fori_loop(0, 2, encode_step, 0)
    first_span(msg, q_send).wait()
    send_group(2)
    lax.fori_loop(2, 4, encode_step, 0)
    remote_span(1, msg, q_send).wait()
    send_group(3)

    ring_rest = pl.ds(1, 7)
    pltpu.make_async_copy(ring_in.at[ring_rest], ring_in.at[ring_rest], s_recv.at[0]).wait()
    plane_out[...] = ring_in[...].reshape(8, HDIM)
    plane_in[0:8, :] = plane_out[...]

    def send_plane(k, carry):
        pltpu.make_async_remote_copy(
            src_ref=plane_out, dst_ref=plane_in.at[pl.ds(k * 8, 8), :],
            send_sem=s_send.at[1], recv_sem=s_recv.at[1],
            device_id=plane_peer(k), device_id_type=MESH,
        ).start()
        return carry

    lax.fori_loop(1, 16, send_plane, 0)
    lax.fori_loop(4, 6, encode_step, 0)
    plane_rest = plane_in.at[pl.ds(8, 120), :]
    pltpu.make_async_copy(plane_rest, plane_rest, s_recv.at[1]).wait()

    half_scale = 0.5 * HDIM**-0.5

    def attend_group(grp):
        land_f[...] = land[pl.ds(grp * GSIZE, GSIZE)].astype(F32).reshape(GSIZE * MROWS, HDIM)
        lane = lax.broadcasted_iota(jnp.int32, (16, HDIM), 1)
        row = lax.broadcasted_iota(jnp.int32, (16, HDIM), 0)
        known = [plane_in[pl.ds(2 * grp + part, 16, stride=8), :] for part in range(2)]
        uid = jnp.concatenate(
            [
                jnp.broadcast_to(
                    jnp.sum(
                        jnp.where(lane == row + 16 * j, known[part], 0.0), axis=1, keepdims=True
                    ),
                    (16, HDIM),
                )
                for j in range(2 * CAP)
                for part in range(2)
            ],
            axis=0,
        )
        for h in range(HEADS):
            query = jnp.concatenate(
                [
                    land_f[pl.ds(cs * 12 + h * CAP + s, GSIZE, stride=MROWS), :]
                    for cs in range(2)
                    for s in range(CAP)
                ],
                axis=0,
            ).astype(BF)
            total = None
            for pair in range(USERS // 2):
                at = slice(pair * 256, pair * 256 + 256)
                score = dot_t(query, kv_v[at, h * HDIM : (h + 1) * HDIM]) * half_scale
                weight = score + score * jnp.tanh(score)
                mine = jnp.concatenate([uid == 2.0 * pair, uid == 2.0 * pair + 1.0], axis=1)
                weight = jnp.where(mine, weight, 0.0).astype(BF)
                part = dot(weight, kv_v[at, HD + h * HDIM : HD + (h + 1) * HDIM])
                total = part if total is None else total + part
            for j in range(2 * CAP):
                row_at = (j // CAP) * 12 + h * CAP + j % CAP
                ret_f[pl.ds(row_at, GSIZE, stride=MROWS), :] = total[
                    j * GSIZE : (j + 1) * GSIZE, :
                ]
        ret_msg[pl.ds(grp * GSIZE, GSIZE)] = ret_f[...].reshape(GSIZE, MROWS, HDIM).astype(BF)

    def send_back(j, carry):
        idx = (j // 32) * 32 + (j % 2) * 16 + (j % 32) // 2
        pltpu.make_async_remote_copy(
            src_ref=ret_msg.at[idx], dst_ref=ret_land.at[idx],
            send_sem=r_send.at[j // 32], recv_sem=r_recv.at[j // 32],
            device_id=peer(idx, -1), device_id_type=MESH,
        ).start()
        return carry

    first_span(land, q_recv).wait()
    attend_group(0)
    ret_land[0] = ret_msg[0]
    lax.fori_loop(1, GSIZE, send_back, 0)

    def group_step(grp, carry):
        remote_span(grp, land, q_recv).wait()
        attend_group(grp)
        lax.fori_loop(grp * GSIZE, grp * GSIZE + GSIZE, send_back, 0)
        return carry

    lax.fori_loop(1, GROUPS, group_step, 0)

    loads[4].wait()

    def own_step(i, carry):
        at = pl.ds(pl.multiple_of(i * 256, 256), 256)
        xn = xn_v[at, :]
        u_v[at, :] = silu(dot(xn, w_v[:, :HD])).astype(BF)
        own_v = silu(dot(xn, w_v[:, HD : 2 * HD])).astype(BF).astype(F32)
        own_k = silu(dot(xn, w_v[:, 3 * HD :])).astype(BF).astype(F32)
        prod = q_v[at, :].astype(F32) * own_k
        for h in range(HEADS):
            lanes = slice(h * HDIM, (h + 1) * HDIM)
            score = jnp.sum(prod[:, lanes], axis=-1, keepdims=True) * half_scale
            weight = (score + score * jnp.tanh(score)).astype(BF).astype(F32)
            att_v[at, lanes] = weight * own_v[:, lanes]
        return carry

    lax.fori_loop(0, 2, own_step, 0)
    place = (grp * 256 + (other * CAP + rank) * 32 + half * 16 + shift).astype(F32)
    place_col = jnp.sum(jnp.where(rows_i == cols_i, place, 0.0), axis=1, keepdims=True)
    lane_slot = lax.broadcasted_iota(jnp.int32, (CAND, GROUPS * 256), 1).astype(F32)
    place_v[...] = jnp.where(lane_slot == place_col, 1.0, 0.0).astype(BF)
    back_v[192:, :] = jnp.zeros((64, HD), BF)

    def hand_on(grp):
        span = pl.ds(grp * GSIZE, GSIZE)
        return pltpu.make_async_remote_copy(
            src_ref=ret_land.at[span], dst_ref=ret_sib.at[span],
            send_sem=f_send.at[grp], recv_sem=f_recv.at[grp],
            device_id=sibling, device_id_type=MESH,
        )

    def unpack(ref, grp, m):
        back_f[...] = ref[pl.ds(grp * GSIZE, GSIZE)].astype(F32).reshape(GSIZE * MROWS, HDIM)
        for s in range(CAP):
            first = (m * CAP + s) * GSIZE
            for h in range(HEADS):
                back_v[first : first + GSIZE, h * HDIM : (h + 1) * HDIM] = back_f[
                    pl.ds(c * 12 + h * CAP + s, GSIZE, stride=MROWS), :
                ].astype(BF)

    def take(grp):
        hand_on(grp).start()
        unpack(ret_land, grp, 0)
        hand_on(grp).wait()
        unpack(ret_sib, grp, 1)

    def gather(grp):
        def gather_step(i, carry):
            at = pl.ds(pl.multiple_of(i * 256, 256), 256)
            slots = pl.ds(pl.multiple_of(grp * 256, 256), 256)
            att_v[at, :] += dot(place_v[at, slots], back_v[...])
            return carry

        lax.fori_loop(0, 2, gather_step, 0)

    first_span(ret_land, r_recv).wait()
    take(0)
    gather(0)

    def take_step(grp, carry):
        remote_span(grp, ret_land, r_recv).wait()
        take(grp)
        gather(grp)
        return carry

    lax.fori_loop(1, GROUPS - 1, take_step, 0)
    remote_span(GROUPS - 1, ret_land, r_recv).wait()
    take(GROUPS - 1)

    def out_step(i, carry):
        at = pl.ds(pl.multiple_of(i * 256, 256), 256)
        last = dot(place_v[at, (GROUPS - 1) * 256 :], back_v[...])
        normed = norm_rows(att_v[at, :] + last).astype(BF).astype(F32)
        out_ref[at, :] = (normed * u_v[at, :].astype(F32)).astype(BF)
        return carry

    lax.fori_loop(0, 2, out_step, 0)

    remote_span(2, msg, q_send).wait()
    remote_span(3, msg, q_send).wait()
    first_span(ret_msg, r_send).wait()

    def sent(grp, carry):
        remote_span(grp, ret_msg, r_send).wait()
        return carry

    lax.fori_loop(1, GROUPS, sent, 0)
    pltpu.make_async_copy(ring_out.at[ring_rest], ring_out.at[ring_rest], s_send.at[0]).wait()
    pltpu.make_async_copy(plane_rest, plane_rest, s_send.at[1]).wait()
    pltpu.make_async_copy(kv_v, kv_hbm, kv_sem).wait()


def write_out(kv_ref, rows_ref, kv_out, rows_out, kv_v, rows_v, in_sem, out_sem):
    spans = [pl.ds(i * 192, 192) for i in range(8)]
    takes = [
        pltpu.make_async_copy(kv_ref.at[span, :], kv_v.at[span, :], in_sem.at[i])
        for i, span in enumerate(spans)
    ]
    puts = [
        pltpu.make_async_copy(kv_v.at[span, :], kv_out.at[span, :], out_sem.at[i])
        for i, span in enumerate(spans)
    ]
    takes.append(pltpu.make_async_copy(rows_ref, rows_v, in_sem.at[8]))
    puts.append(pltpu.make_async_copy(rows_v, rows_out, out_sem.at[8]))
    for take in takes:
        take.start()
    for take, put in zip(takes, puts):
        take.wait()
        put.start()
    for put in puts:
        put.wait()


def body(history, hist_len, cand, cand_owner, cand_user, norm_gain, w_proj):
    any_spec = pl.BlockSpec(memory_space=pl.ANY)
    vmem = pl.BlockSpec(memory_space=pltpu.VMEM)
    dma = pltpu.SemaphoreType.DMA
    results = (
        jax.ShapeDtypeStruct((USERS * ROWS, 2 * HD), BF),
        jax.ShapeDtypeStruct((CAND, HD), BF),
    )
    kv, out = pl.pallas_call(
        kernel,
        out_shape=results,
        in_specs=[
            pl.BlockSpec(memory_space=pltpu.SMEM), vmem, vmem, vmem, any_spec, any_spec, any_spec,
        ],
        out_specs=(any_spec, vmem),
        scratch_shapes=[
            pltpu.VMEM((CAND, D), BF),
            pltpu.VMEM((USERS * ROWS, D), BF),
            pltpu.VMEM((D, 4 * HD), BF),
            pltpu.VMEM((USERS * ROWS, 2 * HD), BF),
            pltpu.VMEM((CAND, D), BF),
            pltpu.VMEM((CAND, HD), BF),
            pltpu.VMEM((CAND, HD), BF),
            pltpu.VMEM((CAND, HD), F32),
            pltpu.VMEM((CAND, GROUPS * 256), BF),
            pltpu.VMEM((CAP, CHIPS, HD), BF),
            pltpu.VMEM((CAP, CHIPS, HD), BF),
            pltpu.VMEM((CHIPS * MROWS, HDIM), F32),
            pltpu.VMEM((CHIPS, MROWS, HDIM), BF),
            pltpu.VMEM((CHIPS, MROWS, HDIM), BF),
            pltpu.VMEM((GSIZE * MROWS, HDIM), F32),
            pltpu.VMEM((GSIZE * MROWS, HDIM), F32),
            pltpu.VMEM((CHIPS, MROWS, HDIM), BF),
            pltpu.VMEM((CHIPS, MROWS, HDIM), BF),
            pltpu.VMEM((CHIPS, MROWS, HDIM), BF),
            pltpu.VMEM((GSIZE * MROWS, HDIM), F32),
            pltpu.VMEM((256, HD), BF),
            pltpu.VMEM((8, HDIM), F32),
            pltpu.VMEM((8, HDIM), F32),
            pltpu.VMEM((8, 1, HDIM), F32),
            pltpu.VMEM((8, 1, HDIM), F32),
            pltpu.VMEM((8, HDIM), F32),
            pltpu.VMEM((HDIM, HDIM), F32),
            dma((6,)),
            dma,
            dma((CAP + 1,)),
            dma((CAP + 1,)),
            pltpu.SemaphoreType.REGULAR,
            dma((GROUPS,)),
            dma((GROUPS,)),
            dma((GROUPS,)),
            dma((GROUPS,)),
            dma((GROUPS,)),
            dma((GROUPS,)),
            dma((2,)),
            dma((2,)),
        ],
        compiler_params=pltpu.CompilerParams(
            collective_id=0, has_side_effects=True, vmem_limit_bytes=56 << 20
        ),
        cost_estimate=pl.CostEstimate(
            flops=12_000_000_000, bytes_accessed=12_000_000, transcendentals=8_000_000
        ),
        name="routed_attention",
    )(
        hist_len,
        cand_owner.reshape(1, CAND),
        cand_user.reshape(1, CAND),
        norm_gain.reshape(1, D),
        cand,
        history.reshape(USERS * ROWS, D),
        w_proj,
    )
    kv, out = pl.pallas_call(
        write_out,
        out_shape=results,
        in_specs=[any_spec, any_spec],
        out_specs=(any_spec, any_spec),
        scratch_shapes=[
            pltpu.VMEM((USERS * ROWS, 2 * HD), BF), pltpu.VMEM((CAND, HD), BF), dma((9,)), dma((9,)),
        ],
        name="write_out",
    )(kv, out)
    return kv.reshape(USERS, ROWS, 2 * HD), out


def solution(mesh):
    placed = (
        P(("grp", "enc"), None, None),
        P(("grp", "enc")),
        P(("grp", "enc"), None),
        P(("grp", "enc"), None),
        P(("grp", "enc")),
        P(),
        P(),
    )
    return jax.shard_map(
        body,
        mesh=mesh,
        in_specs=placed,
        out_specs=(P(("grp", "enc"), None, None), P(("grp", "enc"), None)),
        check_vma=False,
    )
```

time: 73.2 us -> 68 us (0.929)
  local copies, waits for them, and re-layouts: 6.25 us -> 0 us
  Pallas kernels: 66.2 us -> 67.2 us
    unnamed x5 -> x0, local copies, waits for them, and re-layouts: 6.25 us -> none
    pallas_call x1 -> x2, Pallas kernels: 66.2 us -> 67.2 us  [the longest x1 64.1 us: body(): pl.pallas_call(kernel, out_shape=results, in_specs=[pl.BlockSpec(memory_s...]
where the time goes in v2:
time: 68 us; the launch traced here: 67.9 us
  Pallas kernels  67.2 us (99%)
    pallas_call x1, Pallas kernels, body(): pl.pallas_call(kernel, out_shape=results, in_specs=[pl.BlockSpec(memory_s...  64.1 us
    pallas_call x1, Pallas kernels, body(): pl.pallas_call(write_out, out_shape=results, in_specs=[any_spec, any_spec...  3.15 us

profile of v2, /device:TPU:1, one launch (start us, length us, event | category | flops | bytes accessed | tf_op | source)
XLA Modules:
  0.0 67.9 jit_solution(16397852503781200185)
XLA Ops:
  0.6 64.1 %routed_attention.1 = (bf16[1536,1024]{1,0:T(8,128)(2,1)}, bf16[512,512]{1,0:T(8,128)(2,1)}) custom-call(s32[12]{0:T(128)} %len_ref.1, s32[1,512]{1,0:T(1,128)} %bitcast.8, s32[1,512]{1,0:T(1,128)} %bitcast.9, f32[1,1024]{1,0:T(1,128)} %bitcast.7, bf16[512,1024]{1,0:T(8,128)(2,1)} %cand_hbm.1, bf16[1536,1024]{1,0:T(8,128)(2,1)} %bitcast.5, ...), custom_call_target="tpu_custom_call" | custom-call | flops 12000000000 | bytes 12000000 | tf_op jit(solution)/shard_map/routed_attention/pallas_call | solution.py:463
  64.7 3.2 %write_out.1 = (bf16[1536,1024]{1,0:T(8,128)(2,1)}, bf16[512,512]{1,0:T(8,128)(2,1)}) custom-call(bf16[1536,1024]{1,0:T(8,128)(2,1)} %get-tuple-element.6.kv_ref, bf16[512,512]{1,0:T(8,128)(2,1)} %get-tuple-element.7.rows_ref), custom_call_target="tpu_custom_call" | custom-call | tf_op jit(solution)/shard_map/write_out/pallas_call | solution.py:528

commit v3 on v2

--- a/solution.py
+++ b/solution.py
@@ -176,6 +176,20 @@
     for s in range(CAP):
         lay(dot(pick(s), q_v[...]), c, s)
     own_users = slot_users(0)
+    swap_users.wait()
+    ring_out[...] = (own_users + slot_in[...]).reshape(8, 1, HDIM)
+    ring_in[0] = ring_out[0]
+
+    def send_ring(r, carry):
+        pltpu.make_async_remote_copy(
+            src_ref=ring_out.at[r], dst_ref=ring_in.at[r],
+            send_sem=s_send.at[0], recv_sem=s_recv.at[0],
+            device_id=((g + ring_shift(r)) % 8, e), device_id_type=MESH,
+        ).start()
+        return carry
+
+    lax.fori_loop(1, 8, send_ring, 0)
+
     for s in range(CAP):
         swap(s).wait()
         lay(sib_in[s].astype(F32), 1 - c, s)
@@ -200,6 +214,22 @@
     fill(0)
     lax.fori_loop(1, GSIZE, send_query, 0)
     fill(1)
+
+    ring_rest = pl.ds(1, 7)
+    pltpu.make_async_copy(ring_in.at[ring_rest], ring_in.at[ring_rest], s_recv.at[0]).wait()
+    plane_out[...] = ring_in[...].reshape(8, HDIM)
+    plane_in[0:8, :] = plane_out[...]
+
+    def send_plane(k, carry):
+        pltpu.make_async_remote_copy(
+            src_ref=plane_out, dst_ref=plane_in.at[pl.ds(k * 8, 8), :],
+            send_sem=s_send.at[1], recv_sem=s_recv.at[1],
+            device_id=plane_peer(k), device_id_type=MESH,
+        ).start()
+        return carry
+
+    lax.fori_loop(1, 16, send_plane, 0)
+
     send_group(1)
     land[0] = msg[0]
     fill(2)
@@ -214,20 +244,6 @@
         return pltpu.make_async_copy(
             ref.at[pl.ds(1, GSIZE - 1)], ref.at[pl.ds(1, GSIZE - 1)], sem.at[0]
         )
-
-    swap_users.wait()
-    ring_out[...] = (own_users + slot_in[...]).reshape(8, 1, HDIM)
-    ring_in[0] = ring_out[0]
-
-    def send_ring(r, carry):
-        pltpu.make_async_remote_copy(
-            src_ref=ring_out.at[r], dst_ref=ring_in.at[r],
-            send_sem=s_send.at[0], recv_sem=s_recv.at[0],
-            device_id=((g + ring_shift(r)) % 8, e), device_id_type=MESH,
-        ).start()
-        return carry
-
-    lax.fori_loop(1, 8, send_ring, 0)
 
     loads[2].wait()
     loads[3].wait()
@@ -247,28 +263,11 @@
         pltpu.make_async_copy(kv_v.at[at, :], kv_hbm.at[at, :], kv_sem).start()
         return carry
 
-    lax.fori_loop(0, 2, encode_step, 0)
+    send_group(2)
+    send_group(3)
+    lax.fori_loop(0, 6, encode_step, 0)
     first_span(msg, q_send).wait()
-    send_group(2)
-    lax.fori_loop(2, 4, encode_step, 0)
     remote_span(1, msg, q_send).wait()
-    send_group(3)
-
-    ring_rest = pl.ds(1, 7)
-    pltpu.make_async_copy(ring_in.at[ring_rest], ring_in.at[ring_rest], s_recv.at[0]).wait()
-    plane_out[...] = ring_in[...].reshape(8, HDIM)
-    plane_in[0:8, :] = plane_out[...]
-
-    def send_plane(k, carry):
-        pltpu.make_async_remote_copy(
-            src_ref=plane_out, dst_ref=plane_in.at[pl.ds(k * 8, 8), :],
-            send_sem=s_send.at[1], recv_sem=s_recv.at[1],
-            device_id=plane_peer(k), device_id_type=MESH,
-        ).start()
-        return carry
-
-    lax.fori_loop(1, 16, send_plane, 0)
-    lax.fori_loop(4, 6, encode_step, 0)
     plane_rest = plane_in.at[pl.ds(8, 120), :]
     pltpu.make_async_copy(plane_rest, plane_rest, s_recv.at[1]).wait()
 

time: 68 us -> 61.6 us (0.906)
  Pallas kernels: 67.2 us -> 60.8 us
    pallas_call x1, Pallas kernels: 64.1 us -> 57.7 us  [body(): pl.pallas_call(kernel, out_shape=results, in_specs=[pl.BlockSpec(memory_s...]
where the time goes in v3:
time: 61.6 us; the launch traced here: 61.5 us
  Pallas kernels  60.8 us (99%)
  between operations  0.64 us (1%)
    pallas_call x1, Pallas kernels, body(): pl.pallas_call(kernel, out_shape=results, in_specs=[pl.BlockSpec(memory_s...  57.7 us
    pallas_call x1, Pallas kernels, body(): pl.pallas_call(write_out, out_shape=results, in_specs=[any_spec, any_spec...  3.15 us

profile of v3, /device:TPU:1, one launch (start us, length us, event | category | flops | bytes accessed | tf_op | source)
XLA Modules:
  0.0 61.5 jit_solution(18070733674804644613)
XLA Ops:
  0.6 57.7 %routed_attention.1 = (bf16[1536,1024]{1,0:T(8,128)(2,1)}, bf16[512,512]{1,0:T(8,128)(2,1)}) custom-call(s32[12]{0:T(128)} %len_ref.1, s32[1,512]{1,0:T(1,128)} %bitcast.8, s32[1,512]{1,0:T(1,128)} %bitcast.9, f32[1,1024]{1,0:T(1,128)} %bitcast.7, bf16[512,1024]{1,0:T(8,128)(2,1)} %cand_hbm.1, bf16[1536,1024]{1,0:T(8,128)(2,1)} %bitcast.5, ...), custom_call_target="tpu_custom_call" | custom-call | flops 12000000000 | bytes 12000000 | tf_op jit(solution)/shard_map/routed_attention/pallas_call | solution.py:462
  58.3 3.2 %write_out.1 = (bf16[1536,1024]{1,0:T(8,128)(2,1)}, bf16[512,512]{1,0:T(8,128)(2,1)}) custom-call(bf16[1536,1024]{1,0:T(8,128)(2,1)} %get-tuple-element.6.kv_ref, bf16[512,512]{1,0:T(8,128)(2,1)} %get-tuple-element.7.rows_ref), custom_call_target="tpu_custom_call" | custom-call | tf_op jit(solution)/shard_map/write_out/pallas_call | solution.py:527

commit v4 on v3

--- a/solution.py
+++ b/solution.py
@@ -46,11 +46,11 @@
 
 def kernel(
     len_ref, owner_ref, user_ref, gain_ref, cand_hbm, hist_hbm, w_hbm,
-    kv_hbm, out_ref,
-    cand_v, hist_v, w_v, kv_v, xn_v, q_v, u_v, att_v, place_v,
+    kv_v, out_ref,
+    cand_v, hist_v, w_v, xn_v, q_v, u_v, att_v, place_v,
     sib_out, sib_in, tab, msg, land, land_f, ret_f, ret_msg, ret_land, ret_sib, back_f, back_v,
     slot_out, slot_in, ring_out, ring_in, plane_out, plane_in,
-    load_sem, kv_sem, sib_send, sib_recv, ready_sem,
+    load_sem, sib_send, sib_recv, ready_sem,
     q_send, q_recv, r_send, r_recv, f_send, f_recv, s_send, s_recv,
 ):
     g, e = lax.axis_index("grp"), lax.axis_index("enc")
@@ -260,7 +260,6 @@
         kv_v[at, :HD] = jnp.where(live, keys, 0.0).astype(BF)
         values = silu(dot(xn, w_v[:, HD : 2 * HD]))
         kv_v[at, HD:] = jnp.where(live, values, 0.0).astype(BF)
-        pltpu.make_async_copy(kv_v.at[at, :], kv_hbm.at[at, :], kv_sem).start()
         return carry
 
     send_group(2)
@@ -427,50 +426,25 @@
     lax.fori_loop(1, GROUPS, sent, 0)
     pltpu.make_async_copy(ring_out.at[ring_rest], ring_out.at[ring_rest], s_send.at[0]).wait()
     pltpu.make_async_copy(plane_rest, plane_rest, s_send.at[1]).wait()
-    pltpu.make_async_copy(kv_v, kv_hbm, kv_sem).wait()
-
-
-def write_out(kv_ref, rows_ref, kv_out, rows_out, kv_v, rows_v, in_sem, out_sem):
-    spans = [pl.ds(i * 192, 192) for i in range(8)]
-    takes = [
-        pltpu.make_async_copy(kv_ref.at[span, :], kv_v.at[span, :], in_sem.at[i])
-        for i, span in enumerate(spans)
-    ]
-    puts = [
-        pltpu.make_async_copy(kv_v.at[span, :], kv_out.at[span, :], out_sem.at[i])
-        for i, span in enumerate(spans)
-    ]
-    takes.append(pltpu.make_async_copy(rows_ref, rows_v, in_sem.at[8]))
-    puts.append(pltpu.make_async_copy(rows_v, rows_out, out_sem.at[8]))
-    for take in takes:
-        take.start()
-    for take, put in zip(takes, puts):
-        take.wait()
-        put.start()
-    for put in puts:
-        put.wait()
 
 
 def body(history, hist_len, cand, cand_owner, cand_user, norm_gain, w_proj):
     any_spec = pl.BlockSpec(memory_space=pl.ANY)
     vmem = pl.BlockSpec(memory_space=pltpu.VMEM)
     dma = pltpu.SemaphoreType.DMA
-    results = (
-        jax.ShapeDtypeStruct((USERS * ROWS, 2 * HD), BF),
-        jax.ShapeDtypeStruct((CAND, HD), BF),
-    )
     kv, out = pl.pallas_call(
         kernel,
-        out_shape=results,
+        out_shape=(
+            pltpu.VMEM((USERS * ROWS, 2 * HD), BF), pltpu.VMEM((CAND, HD), BF),
+        ),
         in_specs=[
             pl.BlockSpec(memory_space=pltpu.SMEM), vmem, vmem, vmem, any_spec, any_spec, any_spec,
         ],
-        out_specs=(any_spec, vmem),
+        out_specs=(vmem, vmem),
         scratch_shapes=[
             pltpu.VMEM((CAND, D), BF),
             pltpu.VMEM((USERS * ROWS, D), BF),
             pltpu.VMEM((D, 4 * HD), BF),
-            pltpu.VMEM((USERS * ROWS, 2 * HD), BF),
             pltpu.VMEM((CAND, D), BF),
             pltpu.VMEM((CAND, HD), BF),
             pltpu.VMEM((CAND, HD), BF),
@@ -495,7 +469,6 @@
             pltpu.VMEM((8, HDIM), F32),
             pltpu.VMEM((HDIM, HDIM), F32),
             dma((6,)),
-            dma,
             dma((CAP + 1,)),
             dma((CAP + 1,)),
             pltpu.SemaphoreType.REGULAR,
@@ -509,7 +482,7 @@
             dma((2,)),
         ],
         compiler_params=pltpu.CompilerParams(
-            collective_id=0, has_side_effects=True, vmem_limit_bytes=56 << 20
+            collective_id=0, has_side_effects=True, vmem_limit_bytes=58 << 20
         ),
         cost_estimate=pl.CostEstimate(
             flops=12_000_000_000, bytes_accessed=12_000_000, transcendentals=8_000_000
@@ -524,16 +497,6 @@
         history.reshape(USERS * ROWS, D),
         w_proj,
     )
-    kv, out = pl.pallas_call(
-        write_out,
-        out_shape=results,
-        in_specs=[any_spec, any_spec],
-        out_specs=(any_spec, any_spec),
-        scratch_shapes=[
-            pltpu.VMEM((USERS * ROWS, 2 * HD), BF), pltpu.VMEM((CAND, HD), BF), dma((9,)), dma((9,)),
-        ],
-        name="write_out",
-    )(kv, out)
     return kv.reshape(USERS, ROWS, 2 * HD), out
 
 

time: 61.6 us -> 60.1 us (0.976)
  Pallas kernels: 60.8 us -> 56.9 us
  local copies, waits for them, and re-layouts: 0 us -> 2.46 us
    pallas_call x2 -> x1, Pallas kernels: 60.8 us -> 56.9 us  [body(): pl.pallas_call(kernel, out_shape=(pltpu.VMEM((USERS * ROWS, 2 * HD), BF),...]
    unnamed x0 -> x2, local copies, waits for them, and re-layouts: none -> 2.46 us
where the time goes in v4:
time: 60.1 us; the launch traced here: 60 us
  Pallas kernels  56.9 us (95%)
  local copies, waits for them, and re-layouts  2.46 us (4%)
  between operations  0.64 us (1%)
    pallas_call x1, Pallas kernels, body(): pl.pallas_call(kernel, out_shape=(pltpu.VMEM((USERS * ROWS, 2 * HD), BF),...  56.9 us
    unnamed x2, local copies, waits for them, and re-layouts  2.46 us

profile of v4, /device:TPU:1, one launch (start us, length us, event | category | flops | bytes accessed | tf_op | source)
XLA Modules:
  0.0 60.0 jit_solution(11941784984209256385)
XLA Ops:
  0.6 56.9 %routed_attention.1 = (bf16[1536,1024]{1,0:T(8,128)(2,1)S(1)}, bf16[512,512]{1,0:T(8,128)(2,1)S(1)}) custom-call(s32[12]{0:T(128)} %len_ref.1, s32[1,512]{1,0:T(1,128)} %bitcast.8, s32[1,512]{1,0:T(1,128)} %bitcast.9, f32[1,1024]{1,0:T(1,128)} %bitcast.7, bf16[512,1024]{1,0:T(8,128)(2,1)} %cand_hbm.1, bf16[1536,1024]{1,0:T(8,128)(2,1)} %bitcast.6, ...), custom_call_target="tpu_custom_call" | custom-call | flops 12000000000 | bytes 12000000 | tf_op jit(solution)/shard_map/routed_attention/pallas_call | solution.py:435
  57.5 1.7 %copy.11 = bf16[12,128,1024]{2,1,0:T(8,128)(2,1)} copy(bf16[12,128,1024]{2,1,0:T(8,128)(2,1)S(1)} %bitcast.5) | data formatting | bytes 6291456
  59.2 0.8 %copy.12 = bf16[512,512]{1,0:T(8,128)(2,1)} copy(bf16[512,512]{1,0:T(8,128)(2,1)S(1)} %get-tuple-element.7) | data formatting | bytes 1048576

commit v5 on v4

--- a/solution.py
+++ b/solution.py
@@ -78,7 +78,7 @@
             )
         )
     loads.append(pltpu.make_async_copy(hist_hbm, hist_v, load_sem.at[5]))
-    for i in (0, 1, 5, 2, 3, 4):
+    for i in (0, 1):
         loads[i].start()
 
     barrier = pltpu.get_barrier_semaphore()
@@ -132,6 +132,8 @@
     gain = gain_ref[...]
     loads[0].wait()
     loads[1].wait()
+    for i in (5, 2, 3, 4):
+        loads[i].start()
 
     def query_step(i, carry):
         at = pl.ds(pl.multiple_of(i * 256, 256), 256)

time: 60.1 us -> 60.1 us (level)
  no operation moved by 1% of the time
where the time goes in v5:
time: 60.1 us; the launch traced here: 60 us
  Pallas kernels  56.9 us (95%)
  local copies, waits for them, and re-layouts  2.46 us (4%)
  between operations  0.64 us (1%)
    pallas_call x1, Pallas kernels, body(): pl.pallas_call(kernel, out_shape=(pltpu.VMEM((USERS * ROWS, 2 * HD), BF),...  56.9 us
    unnamed x2, local copies, waits for them, and re-layouts  2.46 us

profile of v5, /device:TPU:1, one launch (start us, length us, event | category | flops | bytes accessed | tf_op | source)
XLA Modules:
  0.0 60.0 jit_solution(324450409858977203)
XLA Ops:
  0.6 56.9 %routed_attention.1 = (bf16[1536,1024]{1,0:T(8,128)(2,1)S(1)}, bf16[512,512]{1,0:T(8,128)(2,1)S(1)}) custom-call(s32[12]{0:T(128)} %len_ref.1, s32[1,512]{1,0:T(1,128)} %bitcast.8, s32[1,512]{1,0:T(1,128)} %bitcast.9, f32[1,1024]{1,0:T(1,128)} %bitcast.7, bf16[512,1024]{1,0:T(8,128)(2,1)} %cand_hbm.1, bf16[1536,1024]{1,0:T(8,128)(2,1)} %bitcast.6, ...), custom_call_target="tpu_custom_call" | custom-call | flops 12000000000 | bytes 12000000 | tf_op jit(solution)/shard_map/routed_attention/pallas_call | solution.py:437
  57.5 1.7 %copy.11 = bf16[12,128,1024]{2,1,0:T(8,128)(2,1)} copy(bf16[12,128,1024]{2,1,0:T(8,128)(2,1)S(1)} %bitcast.5) | data formatting | bytes 6291456
  59.2 0.8 %copy.12 = bf16[512,512]{1,0:T(8,128)(2,1)} copy(bf16[512,512]{1,0:T(8,128)(2,1)S(1)} %get-tuple-element.7) | data formatting | bytes 1048576
